TPU v7x, 1024 devices: a whole 8x8x8 slice. The times are simulated.
1024 devices in a mesh: row: 32 (over x, z_hi, core), col: 32 (over y, z_lo).
Axes of the slice: x: 8, y: 8, z: 8 (z_hi: 2, z_lo: 4; z = z_hi * 4 + z_lo), core: 2. Of those that a mesh axis runs over, the one named last changes fastest.
Arguments:
- images: bfloat16 [393216, 1152], P(('row', 'col')), may hold values from -0.1875 to 0.1875
- texts: bfloat16 [393216, 1152], P(('row', 'col')), may hold values from -0.1875 to 0.1875
- labels: int32 [1024, 384], P(('row', 'col')), may hold values from 0 to 383, each once within a row
- logit_scale: float32 [1], replicated, may hold values from 4 to 16
- logit_bias: float32 [1], replicated, may hold values from -3 to -1
Outputs:
- row_loss: float32 [393216], P(('row', 'col'))
- image_grad: bfloat16 [393216, 1152], P(('row', 'col'))
- text_grad: bfloat16 [393216, 1152], P(('row', 'col'))
Inputs may be any that keep to these rules, and one draw needn't show every extreme that they name: Each row of labels is a permutation of 0 to 383.
All inputs are finite; a program needn't handle non-finite values.
Results may differ from a plain program's by a relative error of at most 0.0064.
Values may be sent and summed in bfloat16 or wider, within the bound.
No kernel may reach another device: no remote copies, remote signals or barrier semaphores. Data moves between devices by JAX's collectives and lax.ppermute only.
A program may use at most 32 MiB of HBM per device.

v0:
```python
import jax
import jax.numpy as jnp
from jax import lax
from jax.sharding import PartitionSpec as P


def from_partner(block, axis, distance):
    count = lax.axis_size(axis)
    route = []
    for low in range(count):
        high = low | 1 << distance
        if high != low and high < count:
            route += [(low, high), (high, low)]
    return lax.ppermute(block, axis, route)


def unit_rows(raw):
    values = raw.astype(jnp.float32)
    inv = lax.rsqrt(jnp.sum(values * values, axis=-1, keepdims=True) + 1e-06)
    return ((values * inv).astype(jnp.bfloat16), inv)


def score_block(left, right, scale, bias, signs):
    logits = jnp.dot(left, right.T, preferred_element_type=jnp.float32) * scale + bias
    terms = jax.nn.softplus(-signs * logits)
    weight = (-scale * signs * jax.nn.sigmoid(-signs * logits)).astype(jnp.bfloat16)
    return (jnp.sum(terms, axis=1), weight)


def back_rows(raw, inv, unit_grad):
    values = raw.astype(jnp.float32)
    inner = jnp.sum(values * unit_grad, axis=-1, keepdims=True)
    return (inv * unit_grad - inv * inv * inv * values * inner).astype(jnp.bfloat16)


def transposed(weight, other):
    return lax.dot_general(
        weight, other, (((0,), (0,)), ((), ())), preferred_element_type=jnp.float32
    )


def per_device(images, texts, labels, logit_scale, logit_bias):
    rows_per = images.shape[0]
    scale = logit_scale[0]
    bias = logit_bias[0]
    row_bit = lax.axis_size("row").bit_length() - 2
    col_bit = lax.axis_size("col").bit_length() - 2
    image_unit, image_inv = unit_rows(images)
    text_unit, text_inv = unit_rows(texts)
    column_ids = jnp.arange(rows_per, dtype=jnp.int32)
    own_sign = jnp.where(labels[0][:, None] == column_ids[None, :], 1.0, -1.0).astype(jnp.float32)
    loss_own, weight_own = score_block(image_unit, text_unit, scale, bias, own_sign)
    row_text = from_partner(text_unit, "row", row_bit)
    loss_row, weight_row = score_block(image_unit, row_text, scale, bias, -1.0)
    col_text = from_partner(text_unit, "col", col_bit)
    loss_col, weight_col = score_block(image_unit, col_text, scale, bias, -1.0)
    send_row = transposed(weight_row, image_unit).astype(jnp.bfloat16)
    part_row = from_partner(send_row, "row", row_bit)
    send_col = transposed(weight_col, image_unit).astype(jnp.bfloat16)
    part_col = from_partner(send_col, "col", col_bit)
    image_unit_grad = (
        jnp.dot(weight_own, text_unit, preferred_element_type=jnp.float32)
        + jnp.dot(weight_row, row_text, preferred_element_type=jnp.float32)
        + jnp.dot(weight_col, col_text, preferred_element_type=jnp.float32)
    )
    text_unit_grad = (
        transposed(weight_own, image_unit)
        + part_row.astype(jnp.float32)
        + part_col.astype(jnp.float32)
    )
    row_loss = (loss_own + loss_row + loss_col) / (3.0 * rows_per)
    image_grad = back_rows(images, image_inv, image_unit_grad)
    text_grad = back_rows(texts, text_inv, text_unit_grad)
    return (row_loss, image_grad, text_grad)


def solution(mesh):
    placed = (P(("row", "col"), None), P(("row", "col"), None), P(("row", "col"), None), P(), P())
    return jax.shard_map(
        per_device,
        mesh=mesh,
        in_specs=placed,
        out_specs=(P(("row", "col")), P(("row", "col"), None), P(("row", "col"), None)),
        check_vma=False,
    )
```

profile of v0, /device:TPU:33, one launch (start us, length us, event | category | flops | bytes accessed | tf_op | source)
XLA Modules:
  0.0 110.4 jit_solution(5400405604777361472)
XLA Ops:
  0.6 0.0 copy-start.1
  0.6 0.0 copy-start.4
  0.6 1.5 %fusion.6 = f32[384]{0:T(512)S(1)} fusion(bf16[384,1152]{1,0:T(8,128)(2,1)} %param.6), kind=kLoop, calls=%fused_computation.18 | loop fusion | flops 1326720 | bytes 886272 | tf_op jit(solution)/shard_map/reduce_sum | solution.py:19
  2.2 1.4 %fusion.7 = bf16[384,1152]{1,0:T(8,128)(2,1)S(1)} fusion(bf16[384,1152]{1,0:T(8,128)(2,1)} %param.6, f32[384]{0:T(512)S(1)} %get-tuple-element.4), kind=kLoop, calls=%fused_computation.19 | loop fusion | flops 1327104 | bytes 1771008 | tf_op jit(solution)/shard_map/convert_element_type | solution.py:20
  3.5 6.1 %collective-permute-start.1 = (bf16[384,1152]{1,0:T(8,128)(2,1)S(1)}, bf16[384,1152]{1,0:T(8,128)(2,1)S(1)}, u32[]{:S(2)}, u32[]{:S(2)}) collective-permute-start(bf16[384,1152]{1,0:T(8,128)(2,1)S(1)} %fusion.7), channel_id=1, source_target_pairs={{0,16},{16,0},{1,17},{17,1},{2,18},{18,2},{3,19},{19,3},{4,20},{20... | collective-permute-start | bytes 2654216 | tf_op jit(solution)/shard_map/ppermute | solution.py:14
  9.7 7.1 %collective-permute-start = (bf16[384,1152]{1,0:T(8,128)(2,1)S(1)}, bf16[384,1152]{1,0:T(8,128)(2,1)S(1)}, u32[]{:S(2)}, u32[]{:S(2)}) collective-permute-start(bf16[384,1152]{1,0:T(8,128)(2,1)S(1)} %fusion.7), channel_id=1, source_target_pairs={{0,512},{512,0},{32,544},{544,32},{64,576},{576,64},{96,608},{608,... | collective-permute-start | bytes 2654216 | tf_op jit(solution)/shard_map/ppermute | solution.py:14
  16.8 0.0 copy-done.1
  16.8 0.8 fusion
  18.9 0.0 copy-done.4
  18.9 0.6 reduce
  19.5 0.7 multiply_multiply_fusion.1
  20.2 3.2 %fusion.18 = (f32[384]{0:T(512)}, f32[384,384]{0,1:T(8,128)}) fusion(f32[]{:T(128)} %bitcast.12, f32[]{:T(128)} %bitcast.8, bf16[384,1152]{1,0:T(8,128)(2,1)S(1)} %fusion.7, bf16[384,1152]{1,0:T(8,128)(2,1)S(1)} %copy-done.1, f32[384]{0:T(512)S(1)} %get-tuple-element.6, s32[384]{0:T(512)} %reduce), kind=kOutput, calls=%fused_computation.39 | convolution fusion | flops 342982272 | bytes 2363912 | tf_op jit(solution)/shard_map/dot_general | solution.py:24
  23.4 1.8 %fusion.23 = f32[384,1152]{1,0:T(8,128)S(1)} fusion(bf16[384,1152]{1,0:T(8,128)(2,1)S(1)} %fusion.7, f32[384,384]{0,1:T(8,128)} %get-tuple-element.10, f32[]{:T(128)S(6)} %neg.32, s32[384]{0:T(512)} %reduce), kind=kOutput, calls=%fused_computation.51 | convolution fusion | flops 340918272 | bytes 3245572 | tf_op jit(solution)/shard_map/dot_general | solution.py:62
  25.2 29.8 %collective-permute-done.1 = bf16[384,1152]{1,0:T(8,128)(2,1)S(1)} collective-permute-done((bf16[384,1152]{1,0:T(8,128)(2,1)S(1)}, bf16[384,1152]{1,0:T(8,128)(2,1)S(1)}, u32[]{:S(2)}, u32[]{:S(2)}) %collective-permute-start.1) | collective-permute-done | bytes 884768 | tf_op jit(solution)/shard_map/ppermute | solution.py:14
  54.9 1.0 fusion.20
  56.0 0.8 convolution_convert_fusion
  56.8 3.9 %collective-permute-start.3 = (bf16[384,1152]{1,0:T(8,128)(2,1)S(1)}, bf16[384,1152]{1,0:T(8,128)(2,1)S(1)}, u32[]{:S(2)}, u32[]{:S(2)}) collective-permute-start(bf16[384,1152]{1,0:T(8,128)(2,1)S(1)} %convolution_convert_fusion), channel_id=1, source_target_pairs={{0,16},{16,0},{1,17},{17,1},{2,18},{18,2},{3,19},{19,3},{4,20},{20... | collective-permute-start | bytes 2654216 | tf_op jit(solution)/shard_map/ppermute | solution.py:14
  60.7 0.0 collective-permute-done
  60.7 1.0 fusion.19
  61.7 0.8 convolution_convert_fusion.1
  62.5 3.0 %collective-permute-start.2 = (bf16[384,1152]{1,0:T(8,128)(2,1)S(1)}, bf16[384,1152]{1,0:T(8,128)(2,1)S(1)}, u32[]{:S(2)}, u32[]{:S(2)}) collective-permute-start(bf16[384,1152]{1,0:T(8,128)(2,1)S(1)} %convolution_convert_fusion.1), channel_id=1, source_target_pairs={{0,512},{512,0},{32,544},{544,32},{64,576},{576,64},{96,608},{608,... | collective-permute-start | bytes 2654216 | tf_op jit(solution)/shard_map/ppermute | solution.py:14
  65.5 0.7 convolution_add_fusion.1
  66.2 0.0 copy-start.3
  66.2 1.0 fusion.5
  67.2 0.0 copy-done.3
  67.2 0.6 add_multiply_fusion
  67.8 1.3 %fusion.4 = bf16[384,1152]{1,0:T(8,128)(2,1)} fusion(bf16[384,1152]{1,0:T(8,128)(2,1)S(1)} %copy-done.1, f32[384,1152]{1,0:T(8,128)S(1)} %get-tuple-element.14, f32[384]{0:T(512)S(1)} %get-tuple-element.13, f32[384]{0:T(512)S(1)} %get-tuple-element.5, f32[384]{0:T(512)S(1)} %get-tuple-element.6), kind=kLoop, calls=%fused_computation.16 | loop fusion | flops 2654208 | bytes 3543552 | tf_op jit(solution)/shard_map/convert_element_type | solution.py:33
  69.1 19.9 %collective-permute-done.3 = bf16[384,1152]{1,0:T(8,128)(2,1)S(1)} collective-permute-done((bf16[384,1152]{1,0:T(8,128)(2,1)S(1)}, bf16[384,1152]{1,0:T(8,128)(2,1)S(1)}, u32[]{:S(2)}, u32[]{:S(2)}) %collective-permute-start.3) | collective-permute-done | bytes 884768 | tf_op jit(solution)/shard_map/ppermute | solution.py:14
  89.1 18.8 %collective-permute-done.2 = bf16[384,1152]{1,0:T(8,128)(2,1)S(1)} collective-permute-done((bf16[384,1152]{1,0:T(8,128)(2,1)S(1)}, bf16[384,1152]{1,0:T(8,128)(2,1)S(1)}, u32[]{:S(2)}, u32[]{:S(2)}) %collective-permute-start.2) | collective-permute-done | bytes 884768 | tf_op jit(solution)/shard_map/ppermute | solution.py:14
  107.9 0.0 copy-done.2
  107.9 1.0 fusion.11
  108.9 1.5 %fusion.10 = bf16[384,1152]{1,0:T(8,128)(2,1)} fusion(bf16[384,1152]{1,0:T(8,128)(2,1)S(1)} %copy-done, f32[384]{0:T(512)S(1)} %get-tuple-element.15, f32[384]{0:T(512)S(1)} %get-tuple-element.3, f32[384]{0:T(512)S(1)} %get-tuple-element.4, bf16[384,1152]{1,0:T(8,128)(2,1)S(1)} %collective-permute-done.3, f32[384,1152]{1,0:T(8,128)S(1)} %get-tuple-element.16, ...), kind=kLoop, calls=%fused_computation.22 | loop fusion | flops 4423680 | bytes 5313024 | tf_op jit(solution)/shard_map/convert_element_type | solution.py:33
  (6 shorter events, 0.0 us)
Async XLA Ops:
  0.6 16.2 %copy-start.1 = (bf16[384,1152]{1,0:T(8,128)(2,1)S(1)}, bf16[384,1152]{1,0:T(8,128)(2,1)}, u32[]{:S(2)}) copy-start(bf16[384,1152]{1,0:T(8,128)(2,1)} %param.5) | copy-start | bytes 2654212
  0.6 18.3 %copy-start.4 = (s32[1,384]{1,0:T(1,128)S(1)}, s32[1,384]{1,0:T(1,128)}, u32[]{:S(2)}) copy-start(s32[1,384]{1,0:T(1,128)} %param.7) | copy-start | bytes 4612
  3.5 51.4 %collective-permute-start.1 = (bf16[384,1152]{1,0:T(8,128)(2,1)S(1)}, bf16[384,1152]{1,0:T(8,128)(2,1)S(1)}, u32[]{:S(2)}, u32[]{:S(2)}) collective-permute-start(bf16[384,1152]{1,0:T(8,128)(2,1)S(1)} %fusion.7), channel_id=1, source_target_pairs={{0,16},{16,0},{1,17},{17,1},{2,18},{18,2},{3,19},{19,3},{4,20},{20... | collective-permute-start | bytes 2654216 | tf_op jit(solution)/shard_map/ppermute | solution.py:14
  9.7 51.0 %collective-permute-start = (bf16[384,1152]{1,0:T(8,128)(2,1)S(1)}, bf16[384,1152]{1,0:T(8,128)(2,1)S(1)}, u32[]{:S(2)}, u32[]{:S(2)}) collective-permute-start(bf16[384,1152]{1,0:T(8,128)(2,1)S(1)} %fusion.7), channel_id=1, source_target_pairs={{0,512},{512,0},{32,544},{544,32},{64,576},{576,64},{96,608},{608,... | collective-permute-start | bytes 2654216 | tf_op jit(solution)/shard_map/ppermute | solution.py:14
  56.8 32.3 %collective-permute-start.3 = (bf16[384,1152]{1,0:T(8,128)(2,1)S(1)}, bf16[384,1152]{1,0:T(8,128)(2,1)S(1)}, u32[]{:S(2)}, u32[]{:S(2)}) collective-permute-start(bf16[384,1152]{1,0:T(8,128)(2,1)S(1)} %convolution_convert_fusion), channel_id=1, source_target_pairs={{0,16},{16,0},{1,17},{17,1},{2,18},{18,2},{3,19},{19,3},{4,20},{20... | collective-permute-start | bytes 2654216 | tf_op jit(solution)/shard_map/ppermute | solution.py:14
  62.5 45.4 %collective-permute-start.2 = (bf16[384,1152]{1,0:T(8,128)(2,1)S(1)}, bf16[384,1152]{1,0:T(8,128)(2,1)S(1)}, u32[]{:S(2)}, u32[]{:S(2)}) collective-permute-start(bf16[384,1152]{1,0:T(8,128)(2,1)S(1)} %convolution_convert_fusion.1), channel_id=1, source_target_pairs={{0,512},{512,0},{32,544},{544,32},{64,576},{576,64},{96,608},{608,... | collective-permute-start | bytes 2654216 | tf_op jit(solution)/shard_map/ppermute | solution.py:14
  66.2 1.0 copy-start.3
  67.8 40.1 %copy-start = (bf16[384,1152]{1,0:T(8,128)(2,1)S(1)}, bf16[384,1152]{1,0:T(8,128)(2,1)}, u32[]{:S(2)}) copy-start(bf16[384,1152]{1,0:T(8,128)(2,1)} %param.6) | copy-start | bytes 2654212
  67.8 40.1 %copy-start.2 = (s32[384]{0:T(512)S(1)}, s32[384]{0:T(512)}, u32[]{:S(2)}) copy-start(s32[384]{0:T(512)} %reduce) | copy-start | bytes 4612
  67.8 40.1 %copy-start.5 = (f32[384,384]{0,1:T(8,128)S(1)}, f32[384,384]{0,1:T(8,128)}, u32[]{:S(2)}) copy-start(f32[384,384]{0,1:T(8,128)} %get-tuple-element.10) | copy-start | bytes 1769476
where the time goes:
time: 111 us; the launch traced here: 110 us
  waiting for transfers between devices  68.5 us (62%)
  starting transfers between devices  20.1 us (18%)
  matrix products  11.2 us (10%)
  other arithmetic  8.43 us (8%)
  between operations  2.06 us (2%)
    ppermute x4, waiting for transfers between devices, from_partner(): return lax.ppermute(block, axis, route)  68.5 us
    ppermute x4, starting transfers between devices, from_partner(): return lax.ppermute(block, axis, route)  20.1 us
    dot_general x3, matrix products, score_block(): jnp.dot(left, right.T, preferred_element_type=jnp.float32) * scale + bias  5.26 us
    convert_element_type x2, other arithmetic, back_rows(): (inv * unit_grad - inv * inv * inv * values * inner).astype(jnp.bfloat16)  2.83 us
    dot_general x3, matrix products, transposed(): lax.dot_general(weight, other, (((0,), (0,)), ((), ())), preferred_elemen...  2.52 us
    reduce_sum x2, other arithmetic, unit_rows(): inv = lax.rsqrt(jnp.sum(values * values, axis=-1, keepdims=True) + 1e-06)  2.33 us
  transfers between devices with their start and end apart: 4, of which 3 were waited for; matrix products, arithmetic and copies ran while one was open for 13% of the time, Pallas kernels for 0%

commit v1 on v0

v1 whole, which is shorter than its diff:
```python
import functools
import jax
import jax.numpy as jnp
from jax import lax
from jax.experimental import pallas as pl
from jax.experimental.pallas import tpu as pltpu
from jax.sharding import PartitionSpec as P


def from_partner(block, axis):
    count = lax.axis_size(axis)
    half = count // 2
    return lax.ppermute(block, axis, [(at, at ^ half) for at in range(count)])


def unit_rows(raw):
    values = raw.astype(jnp.float32)
    inv = lax.rsqrt(jnp.sum(values * values, axis=-1, keepdims=True) + 1e-06)
    return ((values * inv).astype(jnp.bfloat16), inv)


def score_block(left, right, scale, bias, signs):
    logits = jnp.dot(left, right.T, preferred_element_type=jnp.float32) * scale + bias
    terms = jax.nn.softplus(-signs * logits)
    weight = (-scale * signs * jax.nn.sigmoid(-signs * logits)).astype(jnp.bfloat16)
    return (jnp.sum(terms, axis=1), weight)


def back_rows(raw, inv, unit_grad):
    values = raw.astype(jnp.float32)
    inner = jnp.sum(values * unit_grad, axis=-1, keepdims=True)
    return (inv * unit_grad - inv * inv * inv * values * inner).astype(jnp.bfloat16)


def transposed(weight, other):
    return lax.dot_general(
        weight, other, (((0,), (0,)), ((), ())), preferred_element_type=jnp.float32
    )


def cross_part(scale_ref, bias_ref, raw_ref, text_unit):
    scale = scale_ref[0]
    bias = bias_ref[0]
    unit, _ = unit_rows(raw_ref[...])
    dots = lax.dot_general(
        text_unit, unit, (((1,), (1,)), ((), ())), preferred_element_type=jnp.float32
    )
    weight = (scale * jax.nn.sigmoid(dots * scale + bias)).astype(jnp.bfloat16)
    return jnp.dot(weight, unit, preferred_element_type=jnp.float32)


def add_part(scale_ref, bias_ref, raw_ref, unit_ref, total_ref, out_ref):
    out_ref[...] = total_ref[...] + cross_part(scale_ref, bias_ref, raw_ref, unit_ref[...])


def add_last(scale_ref, bias_ref, raw_ref, unit_ref, total_ref, text_ref, inv_ref, out_ref):
    grad = total_ref[...] + cross_part(scale_ref, bias_ref, raw_ref, unit_ref[...])
    out_ref[...] = back_rows(text_ref[...], inv_ref[...], grad)


def call(kernel, out, *args):
    smem = pl.BlockSpec(memory_space=pltpu.SMEM)
    vmem = pl.BlockSpec(memory_space=pltpu.VMEM)
    rows, width = out.shape
    return pl.pallas_call(
        kernel,
        out_shape=out,
        in_specs=[smem, smem] + [vmem] * (len(args) - 2),
        out_specs=vmem,
        compiler_params=pltpu.CompilerParams(vmem_limit_bytes=40 * 1024 * 1024),
        cost_estimate=pl.CostEstimate(
            flops=4 * rows * rows * width,
            bytes_accessed=12 * rows * width,
            transcendentals=2 * rows * rows,
        ),
    )(*args)


def per_device(images, texts, labels, logit_scale, logit_bias):
    rows_per, width = images.shape
    scale = logit_scale[0]
    bias = logit_bias[0]
    row_text = from_partner(texts, "row")
    col_text = from_partner(texts, "col")
    row_image = from_partner(images, "row")
    col_image = from_partner(images, "col")

    image_unit, image_inv = unit_rows(images)
    text_unit, text_inv = unit_rows(texts)
    column_ids = jnp.arange(rows_per, dtype=jnp.int32)
    own_sign = jnp.where(labels[0][:, None] == column_ids[None, :], 1.0, -1.0).astype(jnp.float32)
    loss_own, weight_own = score_block(image_unit, text_unit, scale, bias, own_sign)
    text_total = transposed(weight_own, image_unit)

    row_unit, _ = unit_rows(row_text)
    loss_row, weight_row = score_block(image_unit, row_unit, scale, bias, -1.0)
    col_unit, _ = unit_rows(col_text)
    loss_col, weight_col = score_block(image_unit, col_unit, scale, bias, -1.0)
    image_unit_grad = (
        jnp.dot(weight_own, text_unit, preferred_element_type=jnp.float32)
        + jnp.dot(weight_row, row_unit, preferred_element_type=jnp.float32)
        + jnp.dot(weight_col, col_unit, preferred_element_type=jnp.float32)
    )
    row_loss = (loss_own + loss_row + loss_col) / (3.0 * rows_per)
    image_grad = back_rows(images, image_inv, image_unit_grad)

    wide = jax.ShapeDtypeStruct((rows_per, width), jnp.float32)
    half = jax.ShapeDtypeStruct((rows_per, width), jnp.bfloat16)
    text_total = call(add_part, wide, logit_scale, logit_bias, row_image, text_unit, text_total)
    text_grad = call(
        add_last, half, logit_scale, logit_bias, col_image, text_unit, text_total, texts, text_inv
    )
    return (row_loss, image_grad, text_grad)


def solution(mesh):
    placed = (P(("row", "col"), None), P(("row", "col"), None), P(("row", "col"), None), P(), P())
    return jax.shard_map(
        per_device,
        mesh=mesh,
        in_specs=placed,
        out_specs=(P(("row", "col")), P(("row", "col"), None), P(("row", "col"), None)),
        check_vma=False,
    )
```

time: 111 us -> 170 us (1.53)
  the two profiles are of different devices: /device:TPU:33 before, /device:TPU:834 now
where the time goes in v1:
time: 170 us
  starting transfers between devices  93 us (55%)
  waiting for transfers between devices  49 us (29%)
  matrix products  12.4 us (7%)
  other arithmetic  7.84 us (5%)
  Pallas kernels  4.24 us (2%)
  between operations  2.05 us (1%)
    ppermute x4, starting transfers between devices, from_partner(): return lax.ppermute(block, axis, [(at, at ^ half) for at in range(count)])  93 us
    ppermute x4, waiting for transfers between devices, from_partner(): return lax.ppermute(block, axis, [(at, at ^ half) for at in range(count)])  49 us
    dot_general x3, matrix products, score_block(): jnp.dot(left, right.T, preferred_element_type=jnp.float32) * scale + bias  6.73 us
    reduce_sum x4, other arithmetic, unit_rows(): inv = lax.rsqrt(jnp.sum(values * values, axis=-1, keepdims=True) + 1e-06)  5.69 us
    pallas_call x2, Pallas kernels, call(): pl.pallas_call(kernel, out_shape=out, in_specs=[smem, smem] + [vmem] * (l...  4.24 us
  transfers between devices with their start and end apart: 4, of which 3 were waited for; matrix products, arithmetic and copies ran while one was open for 12% of the time, Pallas kernels for 1%

profile of v1, /device:TPU:834, one launch (start us, length us, event | category | flops | bytes accessed | tf_op | source)
XLA Modules:
  0.0 169.8 jit_solution(8286196205212254342)
XLA Ops:
  0.6 0.0 copy-start
  0.6 0.0 copy-start.3
  0.7 81.3 %collective-permute-start = (bf16[384,1152]{1,0:T(8,128)(2,1)}, bf16[384,1152]{1,0:T(8,128)(2,1)}, u32[]{:S(2)}, u32[]{:S(2)}) collective-permute-start(bf16[384,1152]{1,0:T(8,128)(2,1)} %text_ref.1), channel_id=1, source_target_pairs={{0,512},{32,544},{64,576},{96,608},{128,640},{160,672},{192,704},{... | collective-permute-start | bytes 2654216 | tf_op jit(solution)/shard_map/ppermute | solution.py:13
  82.0 1.9 %collective-permute-start.1 = (bf16[384,1152]{1,0:T(8,128)(2,1)}, bf16[384,1152]{1,0:T(8,128)(2,1)}, u32[]{:S(2)}, u32[]{:S(2)}) collective-permute-start(bf16[384,1152]{1,0:T(8,128)(2,1)} %text_ref.1), channel_id=1, source_target_pairs={{0,16},{1,17},{2,18},{3,19},{4,20},{5,21},{6,22},{7,23},{8,24},{9,... | collective-permute-start | bytes 2654216 | tf_op jit(solution)/shard_map/ppermute | solution.py:13
  83.9 1.9 %collective-permute-start.3 = (bf16[384,1152]{1,0:T(8,128)(2,1)}, bf16[384,1152]{1,0:T(8,128)(2,1)S(1)}, u32[]{:S(2)}, u32[]{:S(2)}) collective-permute-start(bf16[384,1152]{1,0:T(8,128)(2,1)} %param.5), channel_id=1, source_target_pairs={{0,512},{32,544},{64,576},{96,608},{128,640},{160,672},{192,704},{... | collective-permute-start | bytes 2654216 | tf_op jit(solution)/shard_map/ppermute | solution.py:13
  85.9 7.8 %collective-permute-start.2 = (bf16[384,1152]{1,0:T(8,128)(2,1)}, bf16[384,1152]{1,0:T(8,128)(2,1)S(1)}, u32[]{:S(2)}, u32[]{:S(2)}) collective-permute-start(bf16[384,1152]{1,0:T(8,128)(2,1)} %param.5), channel_id=1, source_target_pairs={{0,16},{1,17},{2,18},{3,19},{4,20},{5,21},{6,22},{7,23},{8,24},{9,... | collective-permute-start | bytes 2654216 | tf_op jit(solution)/shard_map/ppermute | solution.py:13
  93.7 1.4 fusion.6
  95.1 1.4 fusion
  96.6 0.0 copy-done
  96.6 0.2 fusion.1.unit_ref
  96.8 0.8 rsqrt.37.inv_ref
  98.9 0.0 copy-done.3
  98.9 2.3 %fusion.18 = (f32[384]{0:T(512)S(1)}, f32[384,384]{0,1:T(8,128)S(1)}) fusion(f32[]{:T(128)} %bitcast.8, f32[]{:T(128)} %bitcast.4, bf16[384,1152]{1,0:T(8,128)(2,1)S(1)} %fusion.1.unit_ref, bf16[384,1152]{1,0:T(8,128)(2,1)} %param.5, f32[384]{0:T(512)S(1)} %get-tuple-element.4, s32[384]{0:T(512)S(1)} %reduce), kind=kOutput, calls=%fused_computation.38 | convolution fusion | flops 342982272 | bytes 2363912 | tf_op jit(solution)/shard_map/dot_general | solution.py:23
  101.2 0.0 copy-start.2
  101.2 0.7 fusion.33
  101.9 0.4 copy-done.2
  102.4 0.8 fusion.31.total_ref
  103.2 37.0 %collective-permute-done = bf16[384,1152]{1,0:T(8,128)(2,1)} collective-permute-done((bf16[384,1152]{1,0:T(8,128)(2,1)}, bf16[384,1152]{1,0:T(8,128)(2,1)}, u32[]{:S(2)}, u32[]{:S(2)}) %collective-permute-start) | collective-permute-done | bytes 884768 | tf_op jit(solution)/shard_map/ppermute | solution.py:13
  140.1 1.4 fusion.2
  141.6 0.0 collective-permute-done.1
  141.6 1.4 fusion.4
  143.0 2.2 %fusion.19 = (f32[384]{0:T(512)S(1)}, f32[384,384]{0,1:T(8,128)S(1)}) fusion(f32[]{:T(128)} %bitcast.10, f32[]{:T(128)} %bitcast.7, bf16[384,1152]{1,0:T(8,128)(2,1)} %collective-permute-done, f32[384]{0:T(512)S(1)} %add_rsqrt_fusion.1, bf16[384,1152]{1,0:T(8,128)(2,1)S(1)} %copy-done.2, f32[384]{0:T(512)S(1)} %get-tuple-element.4), kind=kOutput, calls=%fused_computation.39 | convolution fusion | flops 343719552 | bytes 2363912 | tf_op jit(solution)/shard_map/dot_general | solution.py:23
  145.2 2.2 %fusion.20 = (f32[384]{0:T(512)S(1)}, f32[384,384]{0,1:T(8,128)S(1)}) fusion(f32[]{:T(128)} %bitcast.9, f32[]{:T(128)} %bitcast.6, bf16[384,1152]{1,0:T(8,128)(2,1)} %collective-permute-done.1, f32[384]{0:T(512)S(1)} %add_rsqrt_fusion, bf16[384,1152]{1,0:T(8,128)(2,1)S(1)} %copy-done.2, f32[384]{0:T(512)S(1)} %get-tuple-element.4), kind=kOutput, calls=%fused_computation.40 | convolution fusion | flops 343719552 | bytes 2363912 | tf_op jit(solution)/shard_map/dot_general | solution.py:23
  147.4 2.0 %convolution_add_fusion.1 = f32[384,1152]{1,0:T(8,128)S(1)} fusion(f32[384,1152]{1,0:T(8,128)S(1)} %fusion.33, bf16[384,1152]{1,0:T(8,128)(2,1)} %collective-permute-done, f32[384]{0:T(512)S(1)} %add_rsqrt_fusion.1, f32[384,384]{0,1:T(8,128)S(1)} %get-tuple-element.10, f32[]{:T(128)S(6)} %mul.146), kind=kOutput, calls=%fused_computation.1 | convolution fusion | flops 342245376 | bytes 5015044 | tf_op jit(solution)/shard_map/dot_general | solution.py:101
  149.4 2.2 %fusion.11 = (f32[384]{0:T(512)S(1)}, f32[384,1152]{1,0:T(8,128)S(1)}) fusion(bf16[384,1152]{1,0:T(8,128)(2,1)S(1)} %copy-done.2, f32[384,1152]{1,0:T(8,128)S(1)} %convolution_add_fusion.1, bf16[384,1152]{1,0:T(8,128)(2,1)} %collective-permute-done.1, f32[384]{0:T(512)S(1)} %add_rsqrt_fusion, f32[384,384]{0,1:T(8,128)S(1)} %get-tuple-element.6, f32[]{:T(128)S(6)} %mul.146), kind=kOutput, calls=%fused_computation.23 | convolution fusion | flops 343572096 | bytes 5901316 | tf_op jit(solution)/shard_map/dot_general | solution.py:102
  151.6 7.2 %collective-permute-done.3.raw_ref = bf16[384,1152]{1,0:T(8,128)(2,1)S(1)} collective-permute-done((bf16[384,1152]{1,0:T(8,128)(2,1)}, bf16[384,1152]{1,0:T(8,128)(2,1)S(1)}, u32[]{:S(2)}, u32[]{:S(2)}) %collective-permute-start.3) | collective-permute-done | bytes 884768 | tf_op jit(solution)/shard_map/ppermute | solution.py:13
  158.9 1.5 shard_map.76.total_ref
  160.3 0.6 add_multiply_fusion
  160.9 1.3 fusion.10
  162.2 4.8 %collective-permute-done.2.raw_ref = bf16[384,1152]{1,0:T(8,128)(2,1)S(1)} collective-permute-done((bf16[384,1152]{1,0:T(8,128)(2,1)}, bf16[384,1152]{1,0:T(8,128)(2,1)S(1)}, u32[]{:S(2)}, u32[]{:S(2)}) %collective-permute-start.2) | collective-permute-done | bytes 884768 | tf_op jit(solution)/shard_map/ppermute | solution.py:13
  167.0 0.0 copy-done.1
  167.0 2.8 %shard_map.77 = bf16[384,1152]{1,0:T(8,128)(2,1)} custom-call(f32[1]{0:T(128)} %copy.9.scale_ref, f32[1]{0:T(128)} %copy.10.bias_ref, bf16[384,1152]{1,0:T(8,128)(2,1)S(1)} %collective-permute-done.2.raw_ref, bf16[384,1152]{1,0:T(8,128)(2,1)S(1)} %fusion.1.unit_ref, f32[384,1152]{1,0:T(8,128)S(1)} %shard_map.76.total_ref, bf16[384,1152]{1,0:T(8,128)(2,1)S(1)} %copy-done, ...), custom_call_target="tpu_custom_call" | custom-call | flops 679477248 | bytes 5308416 | tf_op jit(solution)/shard_map/pallas_call | solution.py:65
  (6 shorter events, 0.0 us)
Async XLA Ops:
  0.6 95.9 %copy-start = (bf16[384,1152]{1,0:T(8,128)(2,1)S(1)}, bf16[384,1152]{1,0:T(8,128)(2,1)}, u32[]{:S(2)}) copy-start(bf16[384,1152]{1,0:T(8,128)(2,1)} %text_ref.1) | copy-start | bytes 2654212
  0.6 98.2 %copy-start.3 = (s32[1,384]{1,0:T(1,128)S(1)}, s32[1,384]{1,0:T(1,128)}, u32[]{:S(2)}) copy-start(s32[1,384]{1,0:T(1,128)} %param.7) | copy-start | bytes 4612
  0.7 139.5 %collective-permute-start = (bf16[384,1152]{1,0:T(8,128)(2,1)}, bf16[384,1152]{1,0:T(8,128)(2,1)}, u32[]{:S(2)}, u32[]{:S(2)}) collective-permute-start(bf16[384,1152]{1,0:T(8,128)(2,1)} %text_ref.1), channel_id=1, source_target_pairs={{0,512},{32,544},{64,576},{96,608},{128,640},{160,672},{192,704},{... | collective-permute-start | bytes 2654216 | tf_op jit(solution)/shard_map/ppermute | solution.py:13
  82.0 59.6 %collective-permute-start.1 = (bf16[384,1152]{1,0:T(8,128)(2,1)}, bf16[384,1152]{1,0:T(8,128)(2,1)}, u32[]{:S(2)}, u32[]{:S(2)}) collective-permute-start(bf16[384,1152]{1,0:T(8,128)(2,1)} %text_ref.1), channel_id=1, source_target_pairs={{0,16},{1,17},{2,18},{3,19},{4,20},{5,21},{6,22},{7,23},{8,24},{9,... | collective-permute-start | bytes 2654216 | tf_op jit(solution)/shard_map/ppermute | solution.py:13
  83.9 74.9 %collective-permute-start.3 = (bf16[384,1152]{1,0:T(8,128)(2,1)}, bf16[384,1152]{1,0:T(8,128)(2,1)S(1)}, u32[]{:S(2)}, u32[]{:S(2)}) collective-permute-start(bf16[384,1152]{1,0:T(8,128)(2,1)} %param.5), channel_id=1, source_target_pairs={{0,512},{32,544},{64,576},{96,608},{128,640},{160,672},{192,704},{... | collective-permute-start | bytes 2654216 | tf_op jit(solution)/shard_map/ppermute | solution.py:13
  85.9 81.2 %collective-permute-start.2 = (bf16[384,1152]{1,0:T(8,128)(2,1)}, bf16[384,1152]{1,0:T(8,128)(2,1)S(1)}, u32[]{:S(2)}, u32[]{:S(2)}) collective-permute-start(bf16[384,1152]{1,0:T(8,128)(2,1)} %param.5), channel_id=1, source_target_pairs={{0,16},{1,17},{2,18},{3,19},{4,20},{5,21},{6,22},{7,23},{8,24},{9,... | collective-permute-start | bytes 2654216 | tf_op jit(solution)/shard_map/ppermute | solution.py:13
  101.2 1.2 copy-start.2
  160.9 6.1 %copy-start.1 = (f32[384,1]{1,0:T(8,128)S(1)}, f32[384,1]{1,0:T(8,128)}, u32[]{:S(2)}) copy-start(f32[384,1]{1,0:T(8,128)} %rsqrt.37.inv_ref) | copy-start | bytes 4612

commit v2 on v1

--- a/solution.py
+++ b/solution.py
@@ -80,10 +80,10 @@
     rows_per, width = images.shape
     scale = logit_scale[0]
     bias = logit_bias[0]
+    col_text = from_partner(texts, "col")
     row_text = from_partner(texts, "row")
-    col_text = from_partner(texts, "col")
+    col_image = from_partner(images, "col")
     row_image = from_partner(images, "row")
-    col_image = from_partner(images, "col")
 
     image_unit, image_inv = unit_rows(images)
     text_unit, text_inv = unit_rows(texts)
@@ -92,10 +92,10 @@
     loss_own, weight_own = score_block(image_unit, text_unit, scale, bias, own_sign)
     text_total = transposed(weight_own, image_unit)
 
+    col_unit, _ = unit_rows(col_text)
+    loss_col, weight_col = score_block(image_unit, col_unit, scale, bias, -1.0)
     row_unit, _ = unit_rows(row_text)
     loss_row, weight_row = score_block(image_unit, row_unit, scale, bias, -1.0)
-    col_unit, _ = unit_rows(col_text)
-    loss_col, weight_col = score_block(image_unit, col_unit, scale, bias, -1.0)
     image_unit_grad = (
         jnp.dot(weight_own, text_unit, preferred_element_type=jnp.float32)
         + jnp.dot(weight_row, row_unit, preferred_element_type=jnp.float32)
@@ -106,9 +106,9 @@
 
     wide = jax.ShapeDtypeStruct((rows_per, width), jnp.float32)
     half = jax.ShapeDtypeStruct((rows_per, width), jnp.bfloat16)
-    text_total = call(add_part, wide, logit_scale, logit_bias, row_image, text_unit, text_total)
+    text_total = call(add_part, wide, logit_scale, logit_bias, col_image, text_unit, text_total)
     text_grad = call(
-        add_last, half, logit_scale, logit_bias, col_image, text_unit, text_total, texts, text_inv
+        add_last, half, logit_scale, logit_bias, row_image, text_unit, text_total, texts, text_inv
     )
     return (row_loss, image_grad, text_grad)
 

time: 170 us -> 174 us (1.024)
  waiting for transfers between devices: 49 us -> 52.4 us
    ppermute x4, waiting for transfers between devices: 49 us -> 52.4 us  [from_partner(): return lax.ppermute(block, axis, [(at, at ^ half) for at in range(count)])]
  transfers between devices with their start and end apart: 4 -> 4, of which waited for: 3 -> 2; matrix products, arithmetic and copies ran while one was open for 12% -> 12% of each run, Pallas kernels for 1% -> 1%
where the time goes in v2:
time: 174 us; the launch traced here: 173 us
  starting transfers between devices  93 us (53%)
  waiting for transfers between devices  52.4 us (30%)
  matrix products  12.4 us (7%)
  other arithmetic  7.84 us (5%)
  Pallas kernels  4.23 us (2%)
  between operations  2.05 us (1%)
    ppermute x4, starting transfers between devices, from_partner(): return lax.ppermute(block, axis, [(at, at ^ half) for at in range(count)])  93 us
    ppermute x4, waiting for transfers between devices, from_partner(): return lax.ppermute(block, axis, [(at, at ^ half) for at in range(count)])  52.4 us
    dot_general x3, matrix products, score_block(): jnp.dot(left, right.T, preferred_element_type=jnp.float32) * scale + bias  6.73 us
    reduce_sum x4, other arithmetic, unit_rows(): inv = lax.rsqrt(jnp.sum(values * values, axis=-1, keepdims=True) + 1e-06)  5.69 us
    pallas_call x2, Pallas kernels, call(): pl.pallas_call(kernel, out_shape=out, in_specs=[smem, smem] + [vmem] * (l...  4.23 us
  transfers between devices with their start and end apart: 4, of which 2 were waited for; matrix products, arithmetic and copies ran while one was open for 12% of the time, Pallas kernels for 1%

profile of v2, /device:TPU:834, one launch (start us, length us, event | category | flops | bytes accessed | tf_op | source)
XLA Modules:
  0.0 173.2 jit_solution(1758794991922236833)
XLA Ops:
  0.6 0.0 copy-start
  0.6 0.0 copy-start.3
  0.7 81.3 %collective-permute-start = (bf16[384,1152]{1,0:T(8,128)(2,1)}, bf16[384,1152]{1,0:T(8,128)(2,1)}, u32[]{:S(2)}, u32[]{:S(2)}) collective-permute-start(bf16[384,1152]{1,0:T(8,128)(2,1)} %text_ref.1), channel_id=1, source_target_pairs={{0,512},{32,544},{64,576},{96,608},{128,640},{160,672},{192,704},{... | collective-permute-start | bytes 2654216 | tf_op jit(solution)/shard_map/ppermute | solution.py:13
  82.0 1.9 %collective-permute-start.1 = (bf16[384,1152]{1,0:T(8,128)(2,1)}, bf16[384,1152]{1,0:T(8,128)(2,1)}, u32[]{:S(2)}, u32[]{:S(2)}) collective-permute-start(bf16[384,1152]{1,0:T(8,128)(2,1)} %text_ref.1), channel_id=1, source_target_pairs={{0,16},{1,17},{2,18},{3,19},{4,20},{5,21},{6,22},{7,23},{8,24},{9,... | collective-permute-start | bytes 2654216 | tf_op jit(solution)/shard_map/ppermute | solution.py:13
  83.9 7.8 %collective-permute-start.3 = (bf16[384,1152]{1,0:T(8,128)(2,1)}, bf16[384,1152]{1,0:T(8,128)(2,1)S(1)}, u32[]{:S(2)}, u32[]{:S(2)}) collective-permute-start(bf16[384,1152]{1,0:T(8,128)(2,1)} %param.5), channel_id=1, source_target_pairs={{0,16},{1,17},{2,18},{3,19},{4,20},{5,21},{6,22},{7,23},{8,24},{9,... | collective-permute-start | bytes 2654216 | tf_op jit(solution)/shard_map/ppermute | solution.py:13
  91.8 1.9 %collective-permute-start.2 = (bf16[384,1152]{1,0:T(8,128)(2,1)}, bf16[384,1152]{1,0:T(8,128)(2,1)S(1)}, u32[]{:S(2)}, u32[]{:S(2)}) collective-permute-start(bf16[384,1152]{1,0:T(8,128)(2,1)} %param.5), channel_id=1, source_target_pairs={{0,512},{32,544},{64,576},{96,608},{128,640},{160,672},{192,704},{... | collective-permute-start | bytes 2654216 | tf_op jit(solution)/shard_map/ppermute | solution.py:13
  93.7 1.4 fusion.6
  95.1 1.4 fusion
  96.6 0.0 copy-done
  96.6 0.2 fusion.1.unit_ref
  96.8 0.8 rsqrt.37.inv_ref
  98.9 0.0 copy-done.3
  98.9 2.3 %fusion.18 = (f32[384]{0:T(512)S(1)}, f32[384,384]{0,1:T(8,128)S(1)}) fusion(f32[]{:T(128)} %bitcast.8, f32[]{:T(128)} %bitcast.4, bf16[384,1152]{1,0:T(8,128)(2,1)S(1)} %fusion.1.unit_ref, bf16[384,1152]{1,0:T(8,128)(2,1)} %param.5, f32[384]{0:T(512)S(1)} %get-tuple-element.4, s32[384]{0:T(512)S(1)} %reduce), kind=kOutput, calls=%fused_computation.38 | convolution fusion | flops 342982272 | bytes 2363912 | tf_op jit(solution)/shard_map/dot_general | solution.py:23
  101.2 0.0 copy-start.2
  101.2 0.7 fusion.33
  101.9 0.4 copy-done.2
  102.4 0.8 fusion.31.total_ref
  103.2 37.0 %collective-permute-done = bf16[384,1152]{1,0:T(8,128)(2,1)} collective-permute-done((bf16[384,1152]{1,0:T(8,128)(2,1)}, bf16[384,1152]{1,0:T(8,128)(2,1)}, u32[]{:S(2)}, u32[]{:S(2)}) %collective-permute-start) | collective-permute-done | bytes 884768 | tf_op jit(solution)/shard_map/ppermute | solution.py:13
  140.1 1.4 fusion.2
  141.6 0.0 collective-permute-done.1
  141.6 1.4 fusion.4
  143.0 2.2 %fusion.19 = (f32[384]{0:T(512)S(1)}, f32[384,384]{0,1:T(8,128)S(1)}) fusion(f32[]{:T(128)} %bitcast.10, f32[]{:T(128)} %bitcast.7, bf16[384,1152]{1,0:T(8,128)(2,1)} %collective-permute-done, f32[384]{0:T(512)S(1)} %add_rsqrt_fusion.1, bf16[384,1152]{1,0:T(8,128)(2,1)S(1)} %copy-done.2, f32[384]{0:T(512)S(1)} %get-tuple-element.4), kind=kOutput, calls=%fused_computation.39 | convolution fusion | flops 343719552 | bytes 2363912 | tf_op jit(solution)/shard_map/dot_general | solution.py:23
  145.2 2.2 %fusion.20 = (f32[384]{0:T(512)S(1)}, f32[384,384]{0,1:T(8,128)S(1)}) fusion(f32[]{:T(128)} %bitcast.9, f32[]{:T(128)} %bitcast.6, bf16[384,1152]{1,0:T(8,128)(2,1)} %collective-permute-done.1, f32[384]{0:T(512)S(1)} %add_rsqrt_fusion, bf16[384,1152]{1,0:T(8,128)(2,1)S(1)} %copy-done.2, f32[384]{0:T(512)S(1)} %get-tuple-element.4), kind=kOutput, calls=%fused_computation.40 | convolution fusion | flops 343719552 | bytes 2363912 | tf_op jit(solution)/shard_map/dot_general | solution.py:23
  147.4 2.0 %convolution_add_fusion.1 = f32[384,1152]{1,0:T(8,128)S(1)} fusion(f32[384,1152]{1,0:T(8,128)S(1)} %fusion.33, bf16[384,1152]{1,0:T(8,128)(2,1)} %collective-permute-done, f32[384]{0:T(512)S(1)} %add_rsqrt_fusion.1, f32[384,384]{0,1:T(8,128)S(1)} %get-tuple-element.10, f32[]{:T(128)S(6)} %mul.146), kind=kOutput, calls=%fused_computation.1 | convolution fusion | flops 342245376 | bytes 5015044 | tf_op jit(solution)/shard_map/dot_general | solution.py:101
  149.4 2.2 %fusion.11 = (f32[384]{0:T(512)S(1)}, f32[384,1152]{1,0:T(8,128)S(1)}) fusion(bf16[384,1152]{1,0:T(8,128)(2,1)S(1)} %copy-done.2, f32[384,1152]{1,0:T(8,128)S(1)} %convolution_add_fusion.1, bf16[384,1152]{1,0:T(8,128)(2,1)} %collective-permute-done.1, f32[384]{0:T(512)S(1)} %add_rsqrt_fusion, f32[384,384]{0,1:T(8,128)S(1)} %get-tuple-element.6, f32[]{:T(128)S(6)} %mul.146), kind=kOutput, calls=%fused_computation.23 | convolution fusion | flops 343572096 | bytes 5901316 | tf_op jit(solution)/shard_map/dot_general | solution.py:102
  151.6 15.4 %collective-permute-done.3.raw_ref = bf16[384,1152]{1,0:T(8,128)(2,1)S(1)} collective-permute-done((bf16[384,1152]{1,0:T(8,128)(2,1)}, bf16[384,1152]{1,0:T(8,128)(2,1)S(1)}, u32[]{:S(2)}, u32[]{:S(2)}) %collective-permute-start.3) | collective-permute-done | bytes 884768 | tf_op jit(solution)/shard_map/ppermute | solution.py:13
  167.0 1.5 shard_map.76.total_ref
  168.5 0.6 add_multiply_fusion
  169.1 1.3 fusion.10
  170.4 0.0 collective-permute-done.2.raw_ref
  170.4 0.0 copy-done.1
  170.4 2.8 %shard_map.77 = bf16[384,1152]{1,0:T(8,128)(2,1)} custom-call(f32[1]{0:T(128)} %copy.9.scale_ref, f32[1]{0:T(128)} %copy.10.bias_ref, bf16[384,1152]{1,0:T(8,128)(2,1)S(1)} %collective-permute-done.2.raw_ref, bf16[384,1152]{1,0:T(8,128)(2,1)S(1)} %fusion.1.unit_ref, f32[384,1152]{1,0:T(8,128)S(1)} %shard_map.76.total_ref, bf16[384,1152]{1,0:T(8,128)(2,1)S(1)} %copy-done, ...), custom_call_target="tpu_custom_call" | custom-call | flops 679477248 | bytes 5308416 | tf_op jit(solution)/shard_map/pallas_call | solution.py:65
  (6 shorter events, 0.0 us)
Async XLA Ops:
  0.6 95.9 %copy-start = (bf16[384,1152]{1,0:T(8,128)(2,1)S(1)}, bf16[384,1152]{1,0:T(8,128)(2,1)}, u32[]{:S(2)}) copy-start(bf16[384,1152]{1,0:T(8,128)(2,1)} %text_ref.1) | copy-start | bytes 2654212
  0.6 98.2 %copy-start.3 = (s32[1,384]{1,0:T(1,128)S(1)}, s32[1,384]{1,0:T(1,128)}, u32[]{:S(2)}) copy-start(s32[1,384]{1,0:T(1,128)} %param.7) | copy-start | bytes 4612
  0.7 139.5 %collective-permute-start = (bf16[384,1152]{1,0:T(8,128)(2,1)}, bf16[384,1152]{1,0:T(8,128)(2,1)}, u32[]{:S(2)}, u32[]{:S(2)}) collective-permute-start(bf16[384,1152]{1,0:T(8,128)(2,1)} %text_ref.1), channel_id=1, source_target_pairs={{0,512},{32,544},{64,576},{96,608},{128,640},{160,672},{192,704},{... | collective-permute-start | bytes 2654216 | tf_op jit(solution)/shard_map/ppermute | solution.py:13
  82.0 59.6 %collective-permute-start.1 = (bf16[384,1152]{1,0:T(8,128)(2,1)}, bf16[384,1152]{1,0:T(8,128)(2,1)}, u32[]{:S(2)}, u32[]{:S(2)}) collective-permute-start(bf16[384,1152]{1,0:T(8,128)(2,1)} %text_ref.1), channel_id=1, source_target_pairs={{0,16},{1,17},{2,18},{3,19},{4,20},{5,21},{6,22},{7,23},{8,24},{9,... | collective-permute-start | bytes 2654216 | tf_op jit(solution)/shard_map/ppermute | solution.py:13
  83.9 83.1 %collective-permute-start.3 = (bf16[384,1152]{1,0:T(8,128)(2,1)}, bf16[384,1152]{1,0:T(8,128)(2,1)S(1)}, u32[]{:S(2)}, u32[]{:S(2)}) collective-permute-start(bf16[384,1152]{1,0:T(8,128)(2,1)} %param.5), channel_id=1, source_target_pairs={{0,16},{1,17},{2,18},{3,19},{4,20},{5,21},{6,22},{7,23},{8,24},{9,... | collective-permute-start | bytes 2654216 | tf_op jit(solution)/shard_map/ppermute | solution.py:13
  91.8 78.6 %collective-permute-start.2 = (bf16[384,1152]{1,0:T(8,128)(2,1)}, bf16[384,1152]{1,0:T(8,128)(2,1)S(1)}, u32[]{:S(2)}, u32[]{:S(2)}) collective-permute-start(bf16[384,1152]{1,0:T(8,128)(2,1)} %param.5), channel_id=1, source_target_pairs={{0,512},{32,544},{64,576},{96,608},{128,640},{160,672},{192,704},{... | collective-permute-start | bytes 2654216 | tf_op jit(solution)/shard_map/ppermute | solution.py:13
  101.2 1.2 copy-start.2
  169.1 1.3 copy-start.1

commit v3 on v2

v3 whole, which is shorter than its diff:
```python
import functools
import jax
import jax.numpy as jnp
from jax import lax
from jax.experimental import pallas as pl
from jax.experimental.pallas import tpu as pltpu
from jax.sharding import PartitionSpec as P

STEP = 128


def from_partner(block, axis):
    count = lax.axis_size(axis)
    half = count // 2
    return lax.ppermute(block, axis, [(at, at ^ half) for at in range(count)])


def unit_rows(raw):
    values = raw.astype(jnp.float32)
    inv = lax.rsqrt(jnp.sum(values * values, axis=-1, keepdims=True) + 1e-06)
    return ((values * inv).astype(jnp.bfloat16), inv)


def score_block(left, right, scale, bias, signs):
    logits = jnp.dot(left, right.T, preferred_element_type=jnp.float32) * scale + bias
    terms = jax.nn.softplus(-signs * logits)
    weight = (-scale * signs * jax.nn.sigmoid(-signs * logits)).astype(jnp.bfloat16)
    return (jnp.sum(terms, axis=1), weight)


def back_rows(raw, inv, unit_grad):
    values = raw.astype(jnp.float32)
    inner = jnp.sum(values * unit_grad, axis=-1, keepdims=True)
    return (inv * unit_grad - inv * inv * inv * values * inner).astype(jnp.bfloat16)


def transposed(weight, other):
    return lax.dot_general(
        weight, other, (((0,), (0,)), ((), ())), preferred_element_type=jnp.float32
    )


def plain_weight(dots, scale, bias):
    logits = dots * scale + bias
    return ((scale * jax.nn.sigmoid(logits)).astype(jnp.bfloat16), logits)


def dot_rows(left, right):
    return lax.dot_general(
        left, right, (((1,), (1,)), ((), ())), preferred_element_type=jnp.float32
    )


def image_side(last, scale_ref, bias_ref, raw_ref, unit_ref, loss_ref, total_ref, *rest):
    loss_out, grad_out, other = rest[-3:]
    other[...] = unit_rows(raw_ref[...])[0]
    scale = scale_ref[0]
    bias = bias_ref[0]
    for at in range(0, raw_ref.shape[0], STEP):
        rows = pl.ds(at, STEP)
        weight, logits = plain_weight(dot_rows(unit_ref[rows, :], other[...]), scale, bias)
        terms = jnp.maximum(logits, 0.0) + jnp.log1p(jnp.exp(-jnp.abs(logits)))
        loss = loss_ref[rows, :] + jnp.sum(terms, axis=1, keepdims=True)
        grad = total_ref[rows, :] + jnp.dot(
            weight, other[...], preferred_element_type=jnp.float32
        )
        if last:
            image_ref, inv_ref = rest[:2]
            loss_out[rows, :] = loss / (3.0 * raw_ref.shape[0])
            grad_out[rows, :] = back_rows(image_ref[rows, :], inv_ref[rows, :], grad)
        else:
            loss_out[rows, :] = loss
            grad_out[rows, :] = grad


def text_side(scale_ref, bias_ref, raw_ref, unit_ref, total_ref, out_ref, other):
    other[...] = unit_rows(raw_ref[...])[0]
    for at in range(0, raw_ref.shape[0], STEP):
        rows = pl.ds(at, STEP)
        weight, _ = plain_weight(
            dot_rows(unit_ref[rows, :], other[...]), scale_ref[0], bias_ref[0]
        )
        out_ref[rows, :] = total_ref[rows, :] + jnp.dot(
            weight, other[...], preferred_element_type=jnp.float32
        )


def text_last(
    scale_ref, bias_ref, raw_ref, unit_ref, total_ref, text_ref, inv_ref, out_ref, other, done, sems
):
    other[...] = unit_rows(raw_ref[...])[0]
    copies = []
    for index, at in enumerate(range(0, raw_ref.shape[0], STEP)):
        rows = pl.ds(at, STEP)
        weight, _ = plain_weight(
            dot_rows(unit_ref[rows, :], other[...]), scale_ref[0], bias_ref[0]
        )
        grad = total_ref[rows, :] + jnp.dot(
            weight, other[...], preferred_element_type=jnp.float32
        )
        done[rows, :] = back_rows(text_ref[rows, :], inv_ref[rows, :], grad)
        copies.append(
            pltpu.make_async_copy(done.at[rows, :], out_ref.at[rows, :], sems.at[index])
        )
        copies[-1].start()
    for copy in copies:
        copy.wait()


def call(kernel, out, out_specs, scratch, rows, width, *args):
    smem = pl.BlockSpec(memory_space=pltpu.SMEM)
    vmem = pl.BlockSpec(memory_space=pltpu.VMEM)
    return pl.pallas_call(
        kernel,
        out_shape=out,
        in_specs=[smem, smem] + [vmem] * (len(args) - 2),
        out_specs=out_specs,
        scratch_shapes=[pltpu.VMEM((rows, width), jnp.bfloat16)] + scratch,
        compiler_params=pltpu.CompilerParams(vmem_limit_bytes=40 * 1024 * 1024),
        cost_estimate=pl.CostEstimate(
            flops=4 * rows * rows * width,
            bytes_accessed=12 * rows * width,
            transcendentals=2 * rows * rows,
        ),
    )(*args)


def per_device(images, texts, labels, logit_scale, logit_bias):
    rows_per, width = images.shape
    scale = logit_scale[0]
    bias = logit_bias[0]
    col_text = from_partner(texts, "col")
    row_text = from_partner(texts, "row")
    image_unit, image_inv = unit_rows(images)
    col_image = from_partner(images, "col")
    row_image = from_partner(images, "row")
    text_unit, text_inv = unit_rows(texts)
    column_ids = jnp.arange(rows_per, dtype=jnp.int32)
    own_sign = jnp.where(labels[0][:, None] == column_ids[None, :], 1.0, -1.0).astype(jnp.float32)
    loss, weight_own = score_block(image_unit, text_unit, scale, bias, own_sign)
    loss = loss[:, None]
    image_total = jnp.dot(weight_own, text_unit, preferred_element_type=jnp.float32)
    text_total = transposed(weight_own, image_unit)

    vmem = pl.BlockSpec(memory_space=pltpu.VMEM)
    wide = jax.ShapeDtypeStruct((rows_per, width), jnp.float32)
    half = jax.ShapeDtypeStruct((rows_per, width), jnp.bfloat16)
    line = jax.ShapeDtypeStruct((rows_per, 1), jnp.float32)
    loss, image_total = call(
        functools.partial(image_side, False), (line, wide), (vmem, vmem), [], rows_per, width,
        logit_scale, logit_bias, col_text, image_unit, loss, image_total,
    )
    loss, image_grad = call(
        functools.partial(image_side, True), (line, half), (vmem, vmem), [], rows_per, width,
        logit_scale, logit_bias, row_text, image_unit, loss, image_total, images, image_inv,
    )
    image_grad, text_total = lax.optimization_barrier((image_grad, text_total))
    text_total = call(
        text_side, wide, vmem, [], rows_per, width,
        logit_scale, logit_bias, col_image, text_unit, text_total,
    )
    text_grad = call(
        text_last, half, pl.BlockSpec(memory_space=pl.ANY),
        [pltpu.VMEM((rows_per, width), jnp.bfloat16), pltpu.SemaphoreType.DMA((rows_per // STEP,))],
        rows_per, width,
        logit_scale, logit_bias, row_image, text_unit, text_total, texts, text_inv,
    )
    return (loss[:, 0], image_grad, text_grad)


def solution(mesh):
    placed = (P(("row", "col"), None), P(("row", "col"), None), P(("row", "col"), None), P(), P())
    return jax.shard_map(
        per_device,
        mesh=mesh,
        in_specs=placed,
        out_specs=(P(("row", "col")), P(("row", "col"), None), P(("row", "col"), None)),
        check_vma=False,
    )
```

time: 174 us -> 98.8 us (0.57)
  the two profiles are of different devices: /device:TPU:834 before, /device:TPU:904 now
where the time goes in v3:
time: 98.8 us; the launch traced here: 98.2 us
  waiting for transfers between devices  46.1 us (47%)
  starting transfers between devices  20.1 us (20%)
  Pallas kernels  15.4 us (16%)
  matrix products  5.55 us (6%)
  other arithmetic  4.88 us (5%)
  local copies, waits for them, and re-layouts  4.18 us (4%)
  between operations  2.08 us (2%)
    ppermute x4, waiting for transfers between devices, from_partner(): return lax.ppermute(block, axis, [(at, at ^ half) for at in range(count)])  46.1 us
    ppermute x4, starting transfers between devices, from_partner(): return lax.ppermute(block, axis, [(at, at ^ half) for at in range(count)])  20.1 us
    pallas_call x4, Pallas kernels, call(): pl.pallas_call(kernel, out_shape=out, in_specs=[smem, smem] + [vmem] * (l...  15.4 us
    reduce_sum x2, other arithmetic, unit_rows(): inv = lax.rsqrt(jnp.sum(values * values, axis=-1, keepdims=True) + 1e-06)  2.84 us
    unnamed x16, local copies, waits for them, and re-layouts  2.48 us
  transfers between devices with their start and end apart: 4, of which 4 were waited for; matrix products, arithmetic and copies ran while one was open for 12% of the time, Pallas kernels for 11%

profile of v3, /device:TPU:904, one launch (start us, length us, event | category | flops | bytes accessed | tf_op | source)
XLA Modules:
  0.0 98.2 jit_solution(11083438716742982370)
XLA Ops:
  0.6 0.0 copy-start.1
  0.6 0.0 copy-start
  0.7 8.4 %collective-permute-start.1 = (bf16[384,1152]{1,0:T(8,128)(2,1)}, bf16[384,1152]{1,0:T(8,128)(2,1)}, u32[]{:S(2)}, u32[]{:S(2)}) collective-permute-start(bf16[384,1152]{1,0:T(8,128)(2,1)} %text_ref.1), channel_id=1, source_target_pairs={{0,16},{1,17},{2,18},{3,19},{4,20},{5,21},{6,22},{7,23},{8,24},{9,... | collective-permute-start | bytes 2654216 | tf_op jit(solution)/shard_map/ppermute | solution.py:15
  9.1 2.4 %collective-permute-start = (bf16[384,1152]{1,0:T(8,128)(2,1)}, bf16[384,1152]{1,0:T(8,128)(2,1)}, u32[]{:S(2)}, u32[]{:S(2)}) collective-permute-start(bf16[384,1152]{1,0:T(8,128)(2,1)} %text_ref.1), channel_id=1, source_target_pairs={{0,512},{32,544},{64,576},{96,608},{128,640},{160,672},{192,704},{... | collective-permute-start | bytes 2654216 | tf_op jit(solution)/shard_map/ppermute | solution.py:15
  11.5 1.9 %collective-permute-start.3 = (bf16[384,1152]{1,0:T(8,128)(2,1)}, bf16[384,1152]{1,0:T(8,128)(2,1)}, u32[]{:S(2)}, u32[]{:S(2)}) collective-permute-start(bf16[384,1152]{1,0:T(8,128)(2,1)} %rest_0_.1), channel_id=1, source_target_pairs={{0,16},{1,17},{2,18},{3,19},{4,20},{5,21},{6,22},{7,23},{8,24},{9,... | collective-permute-start | bytes 2654216 | tf_op jit(solution)/shard_map/ppermute | solution.py:15
  13.4 7.3 %collective-permute-start.2 = (bf16[384,1152]{1,0:T(8,128)(2,1)}, bf16[384,1152]{1,0:T(8,128)(2,1)}, u32[]{:S(2)}, u32[]{:S(2)}) collective-permute-start(bf16[384,1152]{1,0:T(8,128)(2,1)} %rest_0_.1), channel_id=1, source_target_pairs={{0,512},{32,544},{64,576},{96,608},{128,640},{160,672},{192,704},{... | collective-permute-start | bytes 2654216 | tf_op jit(solution)/shard_map/ppermute | solution.py:15
  20.8 1.4 %fusion.2 = f32[384]{0:T(512)S(1)} fusion(bf16[384,1152]{1,0:T(8,128)(2,1)} %text_ref.1), kind=kLoop, calls=%fused_computation.6 | loop fusion | flops 1326720 | bytes 886272 | tf_op jit(solution)/shard_map/reduce_sum | solution.py:20
  22.2 1.4 %fusion = f32[384]{0:T(512)S(1)} fusion(bf16[384,1152]{1,0:T(8,128)(2,1)} %rest_0_.1), kind=kLoop, calls=%fused_computation.4 | loop fusion | flops 1326720 | bytes 886272 | tf_op jit(solution)/shard_map/reduce_sum | solution.py:20
  24.9 0.0 copy-done.1
  24.9 0.0 copy-done
  24.9 0.0 copy-start.6
  24.9 0.4 fusion.1
  25.3 0.3 copy-done.6
  25.6 1.8 %fusion.8 = (f32[384]{0:T(512)S(1)}, f32[384,384]{0,1:T(8,128)}) fusion(f32[]{:T(128)} %bitcast.8, f32[]{:T(128)} %bitcast.6, bf16[384,1152]{1,0:T(8,128)(2,1)S(1)} %get-tuple-element.17.unit_ref, bf16[384,1152]{1,0:T(8,128)(2,1)S(1)} %get-tuple-element.18.unit_ref, s32[384]{0:T(512)S(1)} %reduce), kind=kOutput, calls=%fused_computation.16 | convolution fusion | flops 341655168 | bytes 2362376 | tf_op jit(solution)/shard_map/dot_general | solution.py:25
  27.5 0.8 rsqrt.14.rest_1_
  28.2 0.8 rsqrt.15.inv_ref
  29.0 0.1 broadcast_in_dim.17.loss_ref
  29.2 0.0 copy-start.7
  29.2 1.8 %fusion.11.total_ref = f32[384,1152]{1,0:T(8,128)S(1)} fusion(bf16[384,1152]{1,0:T(8,128)(2,1)S(1)} %get-tuple-element.18.unit_ref, f32[384,384]{0,1:T(8,128)} %get-tuple-element.16, f32[]{:T(128)S(6)} %neg.16, s32[384]{0:T(512)S(1)} %reduce), kind=kOutput, calls=%fused_computation.21 | convolution fusion | flops 340918272 | bytes 3245572 | tf_op jit(solution)/shard_map/dot_general | solution.py:142
  31.0 1.9 %fusion.9.total_ref = f32[384,1152]{1,0:T(8,128)} fusion(bf16[384,1152]{1,0:T(8,128)(2,1)S(1)} %get-tuple-element.17.unit_ref, f32[384,384]{0,1:T(8,128)S(1)} %copy-done.7, f32[]{:T(128)S(6)} %neg.16, s32[384]{0:T(512)S(1)} %reduce), kind=kOutput, calls=%fused_computation.20 | convolution fusion | flops 340918272 | bytes 3245572 | tf_op jit(solution)/shard_map/dot_general | solution.py:38
  32.9 5.2 %collective-permute-done.1.raw_ref = bf16[384,1152]{1,0:T(8,128)(2,1)} collective-permute-done((bf16[384,1152]{1,0:T(8,128)(2,1)}, bf16[384,1152]{1,0:T(8,128)(2,1)}, u32[]{:S(2)}, u32[]{:S(2)}) %collective-permute-start.1) | collective-permute-done | bytes 884768 | tf_op jit(solution)/shard_map/ppermute | solution.py:15
  38.1 3.4 %shard_map.76 = (f32[384,1]{1,0:T(8,128)S(1)}, f32[384,1152]{1,0:T(8,128)S(1)}) custom-call(f32[1]{0:T(128)} %copy.11.scale_ref, f32[1]{0:T(128)} %copy.12.bias_ref, bf16[384,1152]{1,0:T(8,128)(2,1)} %collective-permute-done.1.raw_ref, bf16[384,1152]{1,0:T(8,128)(2,1)S(1)} %get-tuple-element.17.unit_ref, f32[384,1]{1,0:T(8,128)S(1)} %broadcast_in_dim.17.loss_ref, ...), custom_call_target="tpu_custom_call" | custom-call | flops 679477248 | bytes 5308416 | tf_op jit(solution)/shard_map/pallas_call | solution.py:113
  41.5 9.8 %collective-permute-done.raw_ref = bf16[384,1152]{1,0:T(8,128)(2,1)} collective-permute-done((bf16[384,1152]{1,0:T(8,128)(2,1)}, bf16[384,1152]{1,0:T(8,128)(2,1)}, u32[]{:S(2)}, u32[]{:S(2)}) %collective-permute-start) | collective-permute-done | bytes 884768 | tf_op jit(solution)/shard_map/ppermute | solution.py:15
  51.2 0.0 copy-done.4
  51.2 4.5 %shard_map.77 = (f32[384,1]{1,0:T(8,128)S(1)}, bf16[384,1152]{1,0:T(8,128)(2,1)}) custom-call(f32[1]{0:T(128)} %copy.11.scale_ref, f32[1]{0:T(128)} %copy.12.bias_ref, bf16[384,1152]{1,0:T(8,128)(2,1)} %collective-permute-done.raw_ref, bf16[384,1152]{1,0:T(8,128)(2,1)S(1)} %get-tuple-element.17.unit_ref, f32[384,1]{1,0:T(8,128)S(1)} %get-tuple-element.9.loss_ref, ...), custom_call_target="tpu_custom_call" | custom-call | flops 679477248 | bytes 5308416 | tf_op jit(solution)/shard_map/pallas_call | solution.py:113
  55.8 0.7 copy-done.5
  56.4 1.7 %reduce.1 = f32[384]{0:T(512)} reduce(f32[384,1]{1,0:T(8,128)} %copy-done.5, f32[]{:T(128)} %constant.15), dimensions={1}, to_apply=%get-tuple-element.11.reduce_sub_computation | reduce | bytes 3076 | tf_op jit(solution)/shard_map/pallas_call | solution.py:113
  58.1 27.2 %collective-permute-done.3.raw_ref = bf16[384,1152]{1,0:T(8,128)(2,1)} collective-permute-done((bf16[384,1152]{1,0:T(8,128)(2,1)}, bf16[384,1152]{1,0:T(8,128)(2,1)}, u32[]{:S(2)}, u32[]{:S(2)}) %collective-permute-start.3) | collective-permute-done | bytes 884768 | tf_op jit(solution)/shard_map/ppermute | solution.py:15
  85.3 1.5 %copy-done.2 = f32[384,1152]{1,0:T(8,128)S(1)} copy-done((f32[384,1152]{1,0:T(8,128)S(1)}, f32[384,1152]{1,0:T(8,128)}, u32[]{:S(2)}) %copy-start.2) | copy-done | bytes 1769496
  86.8 3.3 %shard_map.78.total_ref = f32[384,1152]{1,0:T(8,128)S(1)} custom-call(f32[1]{0:T(128)} %copy.11.scale_ref, f32[1]{0:T(128)} %copy.12.bias_ref, bf16[384,1152]{1,0:T(8,128)(2,1)} %collective-permute-done.3.raw_ref, bf16[384,1152]{1,0:T(8,128)(2,1)S(1)} %get-tuple-element.18.unit_ref, f32[384,1152]{1,0:T(8,128)S(1)} %copy-done.2), custom_call_target="tpu_custom_call" | custom-call | flops 679477248 | bytes 5308416 | tf_op jit(solution)/shard_map/pallas_call | solution.py:113
  90.0 4.0 %collective-permute-done.2.raw_ref = bf16[384,1152]{1,0:T(8,128)(2,1)} collective-permute-done((bf16[384,1152]{1,0:T(8,128)(2,1)}, bf16[384,1152]{1,0:T(8,128)(2,1)}, u32[]{:S(2)}, u32[]{:S(2)}) %collective-permute-start.2) | collective-permute-done | bytes 884768 | tf_op jit(solution)/shard_map/ppermute | solution.py:15
  94.0 4.2 %shard_map.79 = bf16[384,1152]{1,0:T(8,128)(2,1)} custom-call(f32[1]{0:T(128)} %copy.11.scale_ref, f32[1]{0:T(128)} %copy.12.bias_ref, bf16[384,1152]{1,0:T(8,128)(2,1)} %collective-permute-done.2.raw_ref, bf16[384,1152]{1,0:T(8,128)(2,1)S(1)} %get-tuple-element.18.unit_ref, f32[384,1152]{1,0:T(8,128)S(1)} %shard_map.78.total_ref, ...), custom_call_target="tpu_custom_call" | custom-call | flops 679477248 | bytes 5308416 | tf_op jit(solution)/shard_map/pallas_call | solution.py:113
  (9 shorter events, 0.0 us)
Async XLA Ops:
  0.6 24.3 %copy-start.1 = (bf16[384,1152]{1,0:T(8,128)(2,1)S(1)}, bf16[384,1152]{1,0:T(8,128)(2,1)}, u32[]{:S(2)}) copy-start(bf16[384,1152]{1,0:T(8,128)(2,1)} %text_ref.1) | copy-start | bytes 2654212
  0.6 24.3 %copy-start = (bf16[384,1152]{1,0:T(8,128)(2,1)S(1)}, bf16[384,1152]{1,0:T(8,128)(2,1)}, u32[]{:S(2)}) copy-start(bf16[384,1152]{1,0:T(8,128)(2,1)} %rest_0_.1) | copy-start | bytes 2654212
  0.7 37.4 %collective-permute-start.1 = (bf16[384,1152]{1,0:T(8,128)(2,1)}, bf16[384,1152]{1,0:T(8,128)(2,1)}, u32[]{:S(2)}, u32[]{:S(2)}) collective-permute-start(bf16[384,1152]{1,0:T(8,128)(2,1)} %text_ref.1), channel_id=1, source_target_pairs={{0,16},{1,17},{2,18},{3,19},{4,20},{5,21},{6,22},{7,23},{8,24},{9,... | collective-permute-start | bytes 2654216 | tf_op jit(solution)/shard_map/ppermute | solution.py:15
  9.1 42.2 %collective-permute-start = (bf16[384,1152]{1,0:T(8,128)(2,1)}, bf16[384,1152]{1,0:T(8,128)(2,1)}, u32[]{:S(2)}, u32[]{:S(2)}) collective-permute-start(bf16[384,1152]{1,0:T(8,128)(2,1)} %text_ref.1), channel_id=1, source_target_pairs={{0,512},{32,544},{64,576},{96,608},{128,640},{160,672},{192,704},{... | collective-permute-start | bytes 2654216 | tf_op jit(solution)/shard_map/ppermute | solution.py:15
  11.5 73.8 %collective-permute-start.3 = (bf16[384,1152]{1,0:T(8,128)(2,1)}, bf16[384,1152]{1,0:T(8,128)(2,1)}, u32[]{:S(2)}, u32[]{:S(2)}) collective-permute-start(bf16[384,1152]{1,0:T(8,128)(2,1)} %rest_0_.1), channel_id=1, source_target_pairs={{0,16},{1,17},{2,18},{3,19},{4,20},{5,21},{6,22},{7,23},{8,24},{9,... | collective-permute-start | bytes 2654216 | tf_op jit(solution)/shard_map/ppermute | solution.py:15
  13.4 80.6 %collective-permute-start.2 = (bf16[384,1152]{1,0:T(8,128)(2,1)}, bf16[384,1152]{1,0:T(8,128)(2,1)}, u32[]{:S(2)}, u32[]{:S(2)}) collective-permute-start(bf16[384,1152]{1,0:T(8,128)(2,1)} %rest_0_.1), channel_id=1, source_target_pairs={{0,512},{32,544},{64,576},{96,608},{128,640},{160,672},{192,704},{... | collective-permute-start | bytes 2654216 | tf_op jit(solution)/shard_map/ppermute | solution.py:15
  24.9 0.7 copy-start.6
  29.2 1.9 %copy-start.7 = (f32[384,384]{0,1:T(8,128)S(1)}, f32[384,384]{0,1:T(8,128)}, u32[]{:S(2)}) copy-start(f32[384,384]{0,1:T(8,128)} %get-tuple-element.16) | copy-start | bytes 1769476
  32.9 18.3 %copy-start.4 = (f32[384,1]{1,0:T(8,128)S(1)}, f32[384,1]{1,0:T(8,128)}, u32[]{:S(2)}) copy-start(f32[384,1]{1,0:T(8,128)} %rsqrt.14.rest_1_) | copy-start | bytes 4612
  55.8 0.7 copy-start.5
  85.3 1.5 %copy-start.2 = (f32[384,1152]{1,0:T(8,128)S(1)}, f32[384,1152]{1,0:T(8,128)}, u32[]{:S(2)}) copy-start(f32[384,1152]{1,0:T(8,128)} %fusion.9.total_ref) | copy-start | bytes 5308420
  86.8 7.3 %copy-start.3 = (f32[384,1]{1,0:T(8,128)S(1)}, f32[384,1]{1,0:T(8,128)}, u32[]{:S(2)}) copy-start(f32[384,1]{1,0:T(8,128)} %rsqrt.15.inv_ref) | copy-start | bytes 4612

commit v4 on v2

--- a/solution.py
+++ b/solution.py
@@ -1,10 +1,11 @@
-import functools
 import jax
 import jax.numpy as jnp
 from jax import lax
 from jax.experimental import pallas as pl
 from jax.experimental.pallas import tpu as pltpu
 from jax.sharding import PartitionSpec as P
+
+STEP = 96
 
 
 def from_partner(block, axis):
@@ -38,35 +39,51 @@
     )
 
 
-def cross_part(scale_ref, bias_ref, raw_ref, text_unit):
-    scale = scale_ref[0]
-    bias = bias_ref[0]
-    unit, _ = unit_rows(raw_ref[...])
-    dots = lax.dot_general(
-        text_unit, unit, (((1,), (1,)), ((), ())), preferred_element_type=jnp.float32
-    )
-    weight = (scale * jax.nn.sigmoid(dots * scale + bias)).astype(jnp.bfloat16)
-    return jnp.dot(weight, unit, preferred_element_type=jnp.float32)
+def plain_weight(dots, scale, bias):
+    return (scale * jax.nn.sigmoid(dots * scale + bias)).astype(jnp.bfloat16)
 
 
-def add_part(scale_ref, bias_ref, raw_ref, unit_ref, total_ref, out_ref):
-    out_ref[...] = total_ref[...] + cross_part(scale_ref, bias_ref, raw_ref, unit_ref[...])
+def dot_rows(left, right):
+    return lax.dot_general(
+        left, right, (((1,), (1,)), ((), ())), preferred_element_type=jnp.float32
+    )
 
 
-def add_last(scale_ref, bias_ref, raw_ref, unit_ref, total_ref, text_ref, inv_ref, out_ref):
-    grad = total_ref[...] + cross_part(scale_ref, bias_ref, raw_ref, unit_ref[...])
-    out_ref[...] = back_rows(text_ref[...], inv_ref[...], grad)
+def cross_part(scale_ref, bias_ref, raw_ref, unit_ref):
+    other = unit_rows(raw_ref[...])[0]
+    weight = plain_weight(dot_rows(unit_ref[...], other), scale_ref[0], bias_ref[0])
+    return jnp.dot(weight, other, preferred_element_type=jnp.float32)
 
 
-def call(kernel, out, *args):
+def text_side(scale_ref, bias_ref, raw_ref, unit_ref, total_ref, out_ref):
+    out_ref[...] = total_ref[...] + cross_part(scale_ref, bias_ref, raw_ref, unit_ref)
+
+
+def text_last(
+    scale_ref, bias_ref, raw_ref, unit_ref, total_ref, text_ref, inv_ref, out_ref, grad, done, sems
+):
+    grad[...] = total_ref[...] + cross_part(scale_ref, bias_ref, raw_ref, unit_ref)
+    copies = []
+    for index, at in enumerate(range(0, grad.shape[0], STEP)):
+        rows = pl.ds(at, STEP)
+        done[rows, :] = back_rows(text_ref[rows, :], inv_ref[rows, :], grad[rows, :])
+        copies.append(
+            pltpu.make_async_copy(done.at[rows, :], out_ref.at[rows, :], sems.at[index])
+        )
+        copies[-1].start()
+    for copy in copies:
+        copy.wait()
+
+
+def call(kernel, out, out_specs, scratch, rows, width, *args):
     smem = pl.BlockSpec(memory_space=pltpu.SMEM)
     vmem = pl.BlockSpec(memory_space=pltpu.VMEM)
-    rows, width = out.shape
     return pl.pallas_call(
         kernel,
         out_shape=out,
         in_specs=[smem, smem] + [vmem] * (len(args) - 2),
-        out_specs=vmem,
+        out_specs=out_specs,
+        scratch_shapes=scratch,
         compiler_params=pltpu.CompilerParams(vmem_limit_bytes=40 * 1024 * 1024),
         cost_estimate=pl.CostEstimate(
             flops=4 * rows * rows * width,
@@ -82,10 +99,9 @@
     bias = logit_bias[0]
     col_text = from_partner(texts, "col")
     row_text = from_partner(texts, "row")
+    image_unit, image_inv = unit_rows(images)
     col_image = from_partner(images, "col")
     row_image = from_partner(images, "row")
-
-    image_unit, image_inv = unit_rows(images)
     text_unit, text_inv = unit_rows(texts)
     column_ids = jnp.arange(rows_per, dtype=jnp.int32)
     own_sign = jnp.where(labels[0][:, None] == column_ids[None, :], 1.0, -1.0).astype(jnp.float32)
@@ -94,21 +110,31 @@
 
     col_unit, _ = unit_rows(col_text)
     loss_col, weight_col = score_block(image_unit, col_unit, scale, bias, -1.0)
+    loss_col, row_text = lax.optimization_barrier((loss_col, row_text))
     row_unit, _ = unit_rows(row_text)
     loss_row, weight_row = score_block(image_unit, row_unit, scale, bias, -1.0)
     image_unit_grad = (
         jnp.dot(weight_own, text_unit, preferred_element_type=jnp.float32)
+        + jnp.dot(weight_col, col_unit, preferred_element_type=jnp.float32)
         + jnp.dot(weight_row, row_unit, preferred_element_type=jnp.float32)
-        + jnp.dot(weight_col, col_unit, preferred_element_type=jnp.float32)
     )
     row_loss = (loss_own + loss_row + loss_col) / (3.0 * rows_per)
     image_grad = back_rows(images, image_inv, image_unit_grad)
 
+    vmem = pl.BlockSpec(memory_space=pltpu.VMEM)
     wide = jax.ShapeDtypeStruct((rows_per, width), jnp.float32)
     half = jax.ShapeDtypeStruct((rows_per, width), jnp.bfloat16)
-    text_total = call(add_part, wide, logit_scale, logit_bias, col_image, text_unit, text_total)
+    image_grad, text_total = lax.optimization_barrier((image_grad, text_total))
+    text_total = call(
+        text_side, wide, vmem, [], rows_per, width,
+        logit_scale, logit_bias, col_image, text_unit, text_total,
+    )
     text_grad = call(
-        add_last, half, logit_scale, logit_bias, row_image, text_unit, text_total, texts, text_inv
+        text_last, half, pl.BlockSpec(memory_space=pl.ANY),
+        [pltpu.VMEM((rows_per, width), jnp.float32), pltpu.VMEM((rows_per, width), jnp.bfloat16),
+         pltpu.SemaphoreType.DMA((rows_per // STEP,))],
+        rows_per, width,
+        logit_scale, logit_bias, row_image, text_unit, text_total, texts, text_inv,
     )
     return (row_loss, image_grad, text_grad)
 

time: 174 us -> 97.1 us (0.56)
  the two profiles are of different devices: /device:TPU:834 before, /device:TPU:904 now
where the time goes in v4:
time: 97.1 us; the launch traced here: 96.5 us
  waiting for transfers between devices  49.1 us (51%)
  starting transfers between devices  20.1 us (21%)
  matrix products  12.6 us (13%)
  other arithmetic  7.85 us (8%)
  Pallas kernels  4.1 us (4%)
  between operations  2.05 us (2%)
    ppermute x4, waiting for transfers between devices, from_partner(): return lax.ppermute(block, axis, [(at, at ^ half) for at in range(count)])  49.1 us
    ppermute x4, starting transfers between devices, from_partner(): return lax.ppermute(block, axis, [(at, at ^ half) for at in range(count)])  20.1 us
    dot_general x3, matrix products, score_block(): jnp.dot(left, right.T, preferred_element_type=jnp.float32) * scale + bias  6.83 us
    reduce_sum x4, other arithmetic, unit_rows(): inv = lax.rsqrt(jnp.sum(values * values, axis=-1, keepdims=True) + 1e-06)  5.69 us
    pallas_call x2, Pallas kernels, call(): pl.pallas_call(kernel, out_shape=out, in_specs=[smem, smem] + [vmem] * (l...  4.1 us
    dot_general x1, matrix products, per_device(): jnp.dot(weight_row, row_unit, preferred_element_type=jnp.float32)  2.21 us
    dot_general x1, matrix products, per_device(): jnp.dot(weight_col, col_unit, preferred_element_type=jnp.float32)  2.01 us
  transfers between devices with their start and end apart: 4, of which 4 were waited for; matrix products, arithmetic and copies ran while one was open for 22% of the time, Pallas kernels for 2%

profile of v4, /device:TPU:904, one launch (start us, length us, event | category | flops | bytes accessed | tf_op | source)
XLA Modules:
  0.0 96.5 jit_solution(11209121028910447745)
XLA Ops:
  0.6 0.0 copy-start
  0.6 0.0 copy-start.3
  0.7 8.4 %collective-permute-start = (bf16[384,1152]{1,0:T(8,128)(2,1)}, bf16[384,1152]{1,0:T(8,128)(2,1)}, u32[]{:S(2)}, u32[]{:S(2)}) collective-permute-start(bf16[384,1152]{1,0:T(8,128)(2,1)} %text_ref.1), channel_id=1, source_target_pairs={{0,16},{1,17},{2,18},{3,19},{4,20},{5,21},{6,22},{7,23},{8,24},{9,... | collective-permute-start | bytes 2654216 | tf_op jit(solution)/shard_map/ppermute | solution.py:14
  9.1 2.4 %collective-permute-start.1 = (bf16[384,1152]{1,0:T(8,128)(2,1)}, bf16[384,1152]{1,0:T(8,128)(2,1)}, u32[]{:S(2)}, u32[]{:S(2)}) collective-permute-start(bf16[384,1152]{1,0:T(8,128)(2,1)} %text_ref.1), channel_id=1, source_target_pairs={{0,512},{32,544},{64,576},{96,608},{128,640},{160,672},{192,704},{... | collective-permute-start | bytes 2654216 | tf_op jit(solution)/shard_map/ppermute | solution.py:14
  11.5 1.9 %collective-permute-start.3 = (bf16[384,1152]{1,0:T(8,128)(2,1)}, bf16[384,1152]{1,0:T(8,128)(2,1)S(1)}, u32[]{:S(2)}, u32[]{:S(2)}) collective-permute-start(bf16[384,1152]{1,0:T(8,128)(2,1)} %param.5), channel_id=1, source_target_pairs={{0,16},{1,17},{2,18},{3,19},{4,20},{5,21},{6,22},{7,23},{8,24},{9,... | collective-permute-start | bytes 2654216 | tf_op jit(solution)/shard_map/ppermute | solution.py:14
  13.4 7.3 %collective-permute-start.2 = (bf16[384,1152]{1,0:T(8,128)(2,1)}, bf16[384,1152]{1,0:T(8,128)(2,1)S(1)}, u32[]{:S(2)}, u32[]{:S(2)}) collective-permute-start(bf16[384,1152]{1,0:T(8,128)(2,1)} %param.5), channel_id=1, source_target_pairs={{0,512},{32,544},{64,576},{96,608},{128,640},{160,672},{192,704},{... | collective-permute-start | bytes 2654216 | tf_op jit(solution)/shard_map/ppermute | solution.py:14
  20.8 1.4 %fusion.6 = f32[384]{0:T(512)S(1)} fusion(bf16[384,1152]{1,0:T(8,128)(2,1)} %param.5), kind=kLoop, calls=%fused_computation.18 | loop fusion | flops 1326720 | bytes 886272 | tf_op jit(solution)/shard_map/reduce_sum | solution.py:19
  22.2 1.4 %fusion = f32[384]{0:T(512)S(1)} fusion(bf16[384,1152]{1,0:T(8,128)(2,1)} %text_ref.1), kind=kLoop, calls=%fused_computation.12 | loop fusion | flops 1326720 | bytes 886272 | tf_op jit(solution)/shard_map/reduce_sum | solution.py:19
  23.6 0.0 copy-done
  23.6 0.2 fusion.1.unit_ref
  23.8 0.8 rsqrt.37.inv_ref
  25.9 0.0 copy-done.3
  26.0 0.0 copy-start.2
  26.0 2.4 %fusion.18 = (f32[384]{0:T(512)S(1)}, f32[384,384]{0,1:T(8,128)S(1)}) fusion(f32[]{:T(128)} %bitcast.8, f32[]{:T(128)} %bitcast.4, bf16[384,1152]{1,0:T(8,128)(2,1)S(1)} %fusion.1.unit_ref, bf16[384,1152]{1,0:T(8,128)(2,1)} %param.5, f32[384]{0:T(512)S(1)} %get-tuple-element.12, s32[384]{0:T(512)S(1)} %reduce), kind=kOutput, calls=%fused_computation.38 | convolution fusion | flops 342982272 | bytes 2363912 | tf_op jit(solution)/shard_map/dot_general | solution.py:24
  28.4 0.0 copy-done.2
  28.4 0.8 fusion.31.total_ref
  29.2 0.7 fusion.33
  29.9 8.2 %collective-permute-done = bf16[384,1152]{1,0:T(8,128)(2,1)} collective-permute-done((bf16[384,1152]{1,0:T(8,128)(2,1)}, bf16[384,1152]{1,0:T(8,128)(2,1)}, u32[]{:S(2)}, u32[]{:S(2)}) %collective-permute-start) | collective-permute-done | bytes 884768 | tf_op jit(solution)/shard_map/ppermute | solution.py:14
  38.1 1.4 %fusion.2 = f32[384]{0:T(512)S(1)} fusion(bf16[384,1152]{1,0:T(8,128)(2,1)} %collective-permute-done), kind=kLoop, calls=%fused_computation.14 | loop fusion | flops 1326720 | bytes 886272 | tf_op jit(solution)/shard_map/reduce_sum | solution.py:19
  39.5 2.2 %fusion.19 = (f32[384]{0:T(512)S(1)}, f32[384,384]{0,1:T(8,128)S(1)}) fusion(f32[]{:T(128)} %bitcast.10, f32[]{:T(128)} %bitcast.7, bf16[384,1152]{1,0:T(8,128)(2,1)} %collective-permute-done, f32[384]{0:T(512)S(1)} %add_rsqrt_fusion.1, bf16[384,1152]{1,0:T(8,128)(2,1)S(1)} %copy-done.2, f32[384]{0:T(512)S(1)} %get-tuple-element.12), kind=kOutput, calls=%fused_computation.39 | convolution fusion | flops 343719552 | bytes 2363912 | tf_op jit(solution)/shard_map/dot_general | solution.py:24
  41.7 9.5 %collective-permute-done.1 = bf16[384,1152]{1,0:T(8,128)(2,1)} collective-permute-done((bf16[384,1152]{1,0:T(8,128)(2,1)}, bf16[384,1152]{1,0:T(8,128)(2,1)}, u32[]{:S(2)}, u32[]{:S(2)}) %collective-permute-start.1) | collective-permute-done | bytes 884768 | tf_op jit(solution)/shard_map/ppermute | solution.py:14
  51.2 1.4 %fusion.4 = f32[384]{0:T(512)S(1)} fusion(bf16[384,1152]{1,0:T(8,128)(2,1)} %collective-permute-done.1), kind=kLoop, calls=%fused_computation.16 | loop fusion | flops 1326720 | bytes 886272 | tf_op jit(solution)/shard_map/reduce_sum | solution.py:19
  52.6 2.2 %fusion.20 = (f32[384]{0:T(512)S(1)}, f32[384,384]{0,1:T(8,128)S(1)}) fusion(f32[]{:T(128)} %bitcast.9, f32[]{:T(128)} %bitcast.6, bf16[384,1152]{1,0:T(8,128)(2,1)} %collective-permute-done.1, f32[384]{0:T(512)S(1)} %add_rsqrt_fusion, bf16[384,1152]{1,0:T(8,128)(2,1)S(1)} %copy-done.2, f32[384]{0:T(512)S(1)} %get-tuple-element.12), kind=kOutput, calls=%fused_computation.40 | convolution fusion | flops 343719552 | bytes 2363912 | tf_op jit(solution)/shard_map/dot_general | solution.py:24
  54.9 2.0 %convolution_add_fusion.1 = f32[384,1152]{1,0:T(8,128)S(1)} fusion(f32[384,1152]{1,0:T(8,128)S(1)} %fusion.33, bf16[384,1152]{1,0:T(8,128)(2,1)} %collective-permute-done, f32[384]{0:T(512)S(1)} %add_rsqrt_fusion.1, f32[384,384]{0,1:T(8,128)S(1)} %get-tuple-element.14, f32[]{:T(128)S(6)} %mul.146), kind=kOutput, calls=%fused_computation.1 | convolution fusion | flops 342245376 | bytes 5015044 | tf_op jit(solution)/shard_map/dot_general | solution.py:118
  56.9 2.2 %fusion.11 = (f32[384]{0:T(512)S(1)}, f32[384,1152]{1,0:T(8,128)S(1)}) fusion(bf16[384,1152]{1,0:T(8,128)(2,1)S(1)} %copy-done.2, f32[384,1152]{1,0:T(8,128)S(1)} %convolution_add_fusion.1, bf16[384,1152]{1,0:T(8,128)(2,1)} %collective-permute-done.1, f32[384]{0:T(512)S(1)} %add_rsqrt_fusion, f32[384,384]{0,1:T(8,128)S(1)} %get-tuple-element.18, f32[]{:T(128)S(6)} %mul.146), kind=kOutput, calls=%fused_computation.23 | convolution fusion | flops 343572096 | bytes 5901316 | tf_op jit(solution)/shard_map/dot_general | solution.py:119
  59.1 1.3 %fusion.10 = bf16[384,1152]{1,0:T(8,128)(2,1)} fusion(bf16[384,1152]{1,0:T(8,128)(2,1)S(1)} %copy-done.2, f32[384,1152]{1,0:T(8,128)S(1)} %get-tuple-element.20, f32[384]{0:T(512)S(1)} %get-tuple-element.19, f32[384]{0:T(512)S(1)} %get-tuple-element.11, f32[384]{0:T(512)S(1)} %get-tuple-element.12), kind=kLoop, calls=%fused_computation.22 | loop fusion | flops 2654208 | bytes 3543552 | tf_op jit(solution)/shard_map/convert_element_type | solution.py:33
  60.4 24.9 %collective-permute-done.3.raw_ref = bf16[384,1152]{1,0:T(8,128)(2,1)S(1)} collective-permute-done((bf16[384,1152]{1,0:T(8,128)(2,1)}, bf16[384,1152]{1,0:T(8,128)(2,1)S(1)}, u32[]{:S(2)}, u32[]{:S(2)}) %collective-permute-start.3) | collective-permute-done | bytes 884768 | tf_op jit(solution)/shard_map/ppermute | solution.py:14
  85.3 1.5 %shard_map.76.total_ref = f32[384,1152]{1,0:T(8,128)S(1)} custom-call(f32[1]{0:T(128)} %copy.9.scale_ref, f32[1]{0:T(128)} %copy.10.bias_ref, bf16[384,1152]{1,0:T(8,128)(2,1)S(1)} %collective-permute-done.3.raw_ref, bf16[384,1152]{1,0:T(8,128)(2,1)S(1)} %fusion.1.unit_ref, f32[384,1152]{1,0:T(8,128)S(1)} %fusion.31.total_ref), custom_call_target="tpu_custom_call" | custom-call | flops 679477248 | bytes 5308416 | tf_op jit(solution)/shard_map/pallas_call | solution.py:81
  86.8 0.6 add_multiply_fusion
  87.4 6.6 %collective-permute-done.2.raw_ref = bf16[384,1152]{1,0:T(8,128)(2,1)S(1)} collective-permute-done((bf16[384,1152]{1,0:T(8,128)(2,1)}, bf16[384,1152]{1,0:T(8,128)(2,1)S(1)}, u32[]{:S(2)}, u32[]{:S(2)}) %collective-permute-start.2) | collective-permute-done | bytes 884768 | tf_op jit(solution)/shard_map/ppermute | solution.py:14
  93.9 0.0 copy-done.1
  93.9 2.6 %shard_map.77 = bf16[384,1152]{1,0:T(8,128)(2,1)} custom-call(f32[1]{0:T(128)} %copy.9.scale_ref, f32[1]{0:T(128)} %copy.10.bias_ref, bf16[384,1152]{1,0:T(8,128)(2,1)S(1)} %collective-permute-done.2.raw_ref, bf16[384,1152]{1,0:T(8,128)(2,1)S(1)} %fusion.1.unit_ref, f32[384,1152]{1,0:T(8,128)S(1)} %shard_map.76.total_ref, bf16[384,1152]{1,0:T(8,128)(2,1)S(1)} %copy-done, ...), custom_call_target="tpu_custom_call" | custom-call | flops 679477248 | bytes 5308416 | tf_op jit(solution)/shard_map/pallas_call | solution.py:81
  (6 shorter events, 0.0 us)
Async XLA Ops:
  0.6 23.0 %copy-start = (bf16[384,1152]{1,0:T(8,128)(2,1)S(1)}, bf16[384,1152]{1,0:T(8,128)(2,1)}, u32[]{:S(2)}) copy-start(bf16[384,1152]{1,0:T(8,128)(2,1)} %text_ref.1) | copy-start | bytes 2654212
  0.6 25.3 %copy-start.3 = (s32[1,384]{1,0:T(1,128)S(1)}, s32[1,384]{1,0:T(1,128)}, u32[]{:S(2)}) copy-start(s32[1,384]{1,0:T(1,128)} %param.7) | copy-start | bytes 4612
  0.7 37.4 %collective-permute-start = (bf16[384,1152]{1,0:T(8,128)(2,1)}, bf16[384,1152]{1,0:T(8,128)(2,1)}, u32[]{:S(2)}, u32[]{:S(2)}) collective-permute-start(bf16[384,1152]{1,0:T(8,128)(2,1)} %text_ref.1), channel_id=1, source_target_pairs={{0,16},{1,17},{2,18},{3,19},{4,20},{5,21},{6,22},{7,23},{8,24},{9,... | collective-permute-start | bytes 2654216 | tf_op jit(solution)/shard_map/ppermute | solution.py:14
  9.1 42.1 %collective-permute-start.1 = (bf16[384,1152]{1,0:T(8,128)(2,1)}, bf16[384,1152]{1,0:T(8,128)(2,1)}, u32[]{:S(2)}, u32[]{:S(2)}) collective-permute-start(bf16[384,1152]{1,0:T(8,128)(2,1)} %text_ref.1), channel_id=1, source_target_pairs={{0,512},{32,544},{64,576},{96,608},{128,640},{160,672},{192,704},{... | collective-permute-start | bytes 2654216 | tf_op jit(solution)/shard_map/ppermute | solution.py:14
  11.5 73.8 %collective-permute-start.3 = (bf16[384,1152]{1,0:T(8,128)(2,1)}, bf16[384,1152]{1,0:T(8,128)(2,1)S(1)}, u32[]{:S(2)}, u32[]{:S(2)}) collective-permute-start(bf16[384,1152]{1,0:T(8,128)(2,1)} %param.5), channel_id=1, source_target_pairs={{0,16},{1,17},{2,18},{3,19},{4,20},{5,21},{6,22},{7,23},{8,24},{9,... | collective-permute-start | bytes 2654216 | tf_op jit(solution)/shard_map/ppermute | solution.py:14
  13.4 80.5 %collective-permute-start.2 = (bf16[384,1152]{1,0:T(8,128)(2,1)}, bf16[384,1152]{1,0:T(8,128)(2,1)S(1)}, u32[]{:S(2)}, u32[]{:S(2)}) collective-permute-start(bf16[384,1152]{1,0:T(8,128)(2,1)} %param.5), channel_id=1, source_target_pairs={{0,512},{32,544},{64,576},{96,608},{128,640},{160,672},{192,704},{... | collective-permute-start | bytes 2654216 | tf_op jit(solution)/shard_map/ppermute | solution.py:14
  26.0 2.4 %copy-start.2 = (bf16[384,1152]{1,0:T(8,128)(2,1)S(1)}, bf16[384,1152]{1,0:T(8,128)(2,1)}, u32[]{:S(2)}) copy-start(bf16[384,1152]{1,0:T(8,128)(2,1)} %param.5) | copy-start | bytes 2654212
  60.4 33.5 %copy-start.1 = (f32[384,1]{1,0:T(8,128)S(1)}, f32[384,1]{1,0:T(8,128)}, u32[]{:S(2)}) copy-start(f32[384,1]{1,0:T(8,128)} %rsqrt.37.inv_ref) | copy-start | bytes 4612

commit v5 on v4

--- a/solution.py
+++ b/solution.py
@@ -5,7 +5,7 @@
 from jax.experimental.pallas import tpu as pltpu
 from jax.sharding import PartitionSpec as P
 
-STEP = 96
+STEP = 128
 
 
 def from_partner(block, axis):
@@ -27,10 +27,14 @@
     return (jnp.sum(terms, axis=1), weight)
 
 
-def back_rows(raw, inv, unit_grad):
+def raw_grad(raw, inv, unit_grad):
     values = raw.astype(jnp.float32)
     inner = jnp.sum(values * unit_grad, axis=-1, keepdims=True)
-    return (inv * unit_grad - inv * inv * inv * values * inner).astype(jnp.bfloat16)
+    return inv * unit_grad - inv * inv * inv * values * inner
+
+
+def back_rows(raw, inv, unit_grad):
+    return raw_grad(raw, inv, unit_grad).astype(jnp.bfloat16)
 
 
 def transposed(weight, other):
@@ -49,24 +53,33 @@
     )
 
 
-def cross_part(scale_ref, bias_ref, raw_ref, unit_ref):
+def cross_weight(scale_ref, bias_ref, raw_ref, unit_ref):
     other = unit_rows(raw_ref[...])[0]
-    weight = plain_weight(dot_rows(unit_ref[...], other), scale_ref[0], bias_ref[0])
-    return jnp.dot(weight, other, preferred_element_type=jnp.float32)
+    dots = dot_rows(unit_ref[...], other)
+    return (other, dots, plain_weight(dots, scale_ref[0], bias_ref[0]))
 
 
-def text_side(scale_ref, bias_ref, raw_ref, unit_ref, total_ref, out_ref):
-    out_ref[...] = total_ref[...] + cross_part(scale_ref, bias_ref, raw_ref, unit_ref)
+def text_side(scale_ref, bias_ref, raw_ref, unit_ref, total_ref, text_ref, inv_ref, out_ref):
+    other, _, weight = cross_weight(scale_ref, bias_ref, raw_ref, unit_ref)
+    grad = total_ref[...] + jnp.dot(weight, other, preferred_element_type=jnp.float32)
+    out_ref[...] = raw_grad(text_ref[...], inv_ref[...], grad)
 
 
 def text_last(
-    scale_ref, bias_ref, raw_ref, unit_ref, total_ref, text_ref, inv_ref, out_ref, grad, done, sems
+    scale_ref, bias_ref, raw_ref, unit_ref, base_ref, text_ref, inv_ref, out_ref, done, sems
 ):
-    grad[...] = total_ref[...] + cross_part(scale_ref, bias_ref, raw_ref, unit_ref)
+    other, dots, weight = cross_weight(scale_ref, bias_ref, raw_ref, unit_ref)
+    inv = inv_ref[...]
+    inner = jnp.sum(weight.astype(jnp.float32) * dots, axis=1, keepdims=True)
+    along = inv * inv * inner
     copies = []
-    for index, at in enumerate(range(0, grad.shape[0], STEP)):
+    for index, at in enumerate(range(0, done.shape[0], STEP)):
         rows = pl.ds(at, STEP)
-        done[rows, :] = back_rows(text_ref[rows, :], inv_ref[rows, :], grad[rows, :])
+        part = jnp.dot(weight[at : at + STEP], other, preferred_element_type=jnp.float32)
+        values = text_ref[rows, :].astype(jnp.float32)
+        done[rows, :] = (
+            base_ref[rows, :] + inv[at : at + STEP] * part - along[at : at + STEP] * values
+        ).astype(jnp.bfloat16)
         copies.append(
             pltpu.make_async_copy(done.at[rows, :], out_ref.at[rows, :], sems.at[index])
         )
@@ -127,12 +140,11 @@
     image_grad, text_total = lax.optimization_barrier((image_grad, text_total))
     text_total = call(
         text_side, wide, vmem, [], rows_per, width,
-        logit_scale, logit_bias, col_image, text_unit, text_total,
+        logit_scale, logit_bias, col_image, text_unit, text_total, texts, text_inv,
     )
     text_grad = call(
         text_last, half, pl.BlockSpec(memory_space=pl.ANY),
-        [pltpu.VMEM((rows_per, width), jnp.float32), pltpu.VMEM((rows_per, width), jnp.bfloat16),
-         pltpu.SemaphoreType.DMA((rows_per // STEP,))],
+        [pltpu.VMEM((rows_per, width), jnp.bfloat16), pltpu.SemaphoreType.DMA((rows_per // STEP,))],
         rows_per, width,
         logit_scale, logit_bias, row_image, text_unit, text_total, texts, text_inv,
     )

time: 97.1 us -> 96.9 us (level)
  Pallas kernels: 4.1 us -> 5.35 us
    pallas_call x2, Pallas kernels: 4.1 us -> 5.35 us  [call(): pl.pallas_call(kernel, out_shape=out, in_specs=[smem, smem] + [vmem] * (l...]
  transfers between devices with their start and end apart: 4 -> 4, of which waited for: 4 -> 4; matrix products, arithmetic and copies ran while one was open for 22% -> 21% of each run, Pallas kernels for 2% -> 3%
where the time goes in v5:
time: 96.9 us; the launch traced here: 96.2 us
  waiting for transfers between devices  48.3 us (50%)
  starting transfers between devices  20.1 us (21%)
  matrix products  12.5 us (13%)
  other arithmetic  7.85 us (8%)
  Pallas kernels  5.35 us (6%)
  between operations  2.06 us (2%)
    ppermute x4, waiting for transfers between devices, from_partner(): return lax.ppermute(block, axis, [(at, at ^ half) for at in range(count)])  48.3 us
    ppermute x4, starting transfers between devices, from_partner(): return lax.ppermute(block, axis, [(at, at ^ half) for at in range(count)])  20.1 us
    dot_general x3, matrix products, score_block(): jnp.dot(left, right.T, preferred_element_type=jnp.float32) * scale + bias  6.82 us
    reduce_sum x4, other arithmetic, unit_rows(): inv = lax.rsqrt(jnp.sum(values * values, axis=-1, keepdims=True) + 1e-06)  5.69 us
    pallas_call x2, Pallas kernels, call(): pl.pallas_call(kernel, out_shape=out, in_specs=[smem, smem] + [vmem] * (l...  5.35 us
    dot_general x1, matrix products, per_device(): jnp.dot(weight_row, row_unit, preferred_element_type=jnp.float32)  2.21 us
    dot_general x1, matrix products, per_device(): jnp.dot(weight_col, col_unit, preferred_element_type=jnp.float32)  1.98 us
  transfers between devices with their start and end apart: 4, of which 4 were waited for; matrix products, arithmetic and copies ran while one was open for 21% of the time, Pallas kernels for 3%

profile of v5, /device:TPU:904, one launch (start us, length us, event | category | flops | bytes accessed | tf_op | source)
XLA Modules:
  0.0 96.2 jit_solution(11639499613276885303)
XLA Ops:
  0.6 0.0 copy-start
  0.6 0.0 copy-start.2
  0.7 8.4 %collective-permute-start = (bf16[384,1152]{1,0:T(8,128)(2,1)}, bf16[384,1152]{1,0:T(8,128)(2,1)}, u32[]{:S(2)}, u32[]{:S(2)}) collective-permute-start(bf16[384,1152]{1,0:T(8,128)(2,1)} %text_ref.3), channel_id=1, source_target_pairs={{0,16},{1,17},{2,18},{3,19},{4,20},{5,21},{6,22},{7,23},{8,24},{9,... | collective-permute-start | bytes 2654216 | tf_op jit(solution)/shard_map/ppermute | solution.py:14
  9.1 2.4 %collective-permute-start.1 = (bf16[384,1152]{1,0:T(8,128)(2,1)}, bf16[384,1152]{1,0:T(8,128)(2,1)}, u32[]{:S(2)}, u32[]{:S(2)}) collective-permute-start(bf16[384,1152]{1,0:T(8,128)(2,1)} %text_ref.3), channel_id=1, source_target_pairs={{0,512},{32,544},{64,576},{96,608},{128,640},{160,672},{192,704},{... | collective-permute-start | bytes 2654216 | tf_op jit(solution)/shard_map/ppermute | solution.py:14
  11.5 1.9 %collective-permute-start.3 = (bf16[384,1152]{1,0:T(8,128)(2,1)}, bf16[384,1152]{1,0:T(8,128)(2,1)}, u32[]{:S(2)}, u32[]{:S(2)}) collective-permute-start(bf16[384,1152]{1,0:T(8,128)(2,1)} %param.5), channel_id=1, source_target_pairs={{0,16},{1,17},{2,18},{3,19},{4,20},{5,21},{6,22},{7,23},{8,24},{9,... | collective-permute-start | bytes 2654216 | tf_op jit(solution)/shard_map/ppermute | solution.py:14
  13.4 7.3 %collective-permute-start.2 = (bf16[384,1152]{1,0:T(8,128)(2,1)}, bf16[384,1152]{1,0:T(8,128)(2,1)S(1)}, u32[]{:S(2)}, u32[]{:S(2)}) collective-permute-start(bf16[384,1152]{1,0:T(8,128)(2,1)} %param.5), channel_id=1, source_target_pairs={{0,512},{32,544},{64,576},{96,608},{128,640},{160,672},{192,704},{... | collective-permute-start | bytes 2654216 | tf_op jit(solution)/shard_map/ppermute | solution.py:14
  20.8 1.4 %fusion.6 = f32[384]{0:T(512)S(1)} fusion(bf16[384,1152]{1,0:T(8,128)(2,1)} %param.5), kind=kLoop, calls=%fused_computation.18 | loop fusion | flops 1326720 | bytes 886272 | tf_op jit(solution)/shard_map/reduce_sum | solution.py:19
  22.2 1.4 %fusion = f32[384]{0:T(512)S(1)} fusion(bf16[384,1152]{1,0:T(8,128)(2,1)} %text_ref.3), kind=kLoop, calls=%fused_computation.12 | loop fusion | flops 1326720 | bytes 886272 | tf_op jit(solution)/shard_map/reduce_sum | solution.py:19
  23.6 0.0 copy-done
  23.6 0.2 fusion.1.unit_ref
  23.8 0.1 rsqrt.37.inv_ref
  25.3 0.0 copy-done.2
  25.3 0.0 copy-start.1
  25.3 2.4 %fusion.18 = (f32[384]{0:T(512)S(1)}, f32[384,384]{0,1:T(8,128)S(1)}) fusion(f32[]{:T(128)} %bitcast.8, f32[]{:T(128)} %bitcast.4, bf16[384,1152]{1,0:T(8,128)(2,1)S(1)} %fusion.1.unit_ref, bf16[384,1152]{1,0:T(8,128)(2,1)} %param.5, f32[384]{0:T(512)S(1)} %get-tuple-element.12, s32[384]{0:T(512)S(1)} %reduce), kind=kOutput, calls=%fused_computation.38 | convolution fusion | flops 342982272 | bytes 2363912 | tf_op jit(solution)/shard_map/dot_general | solution.py:24
  27.7 0.0 copy-done.1
  27.7 0.8 fusion.31.total_ref
  28.5 0.7 fusion.33
  29.2 8.9 %collective-permute-done = bf16[384,1152]{1,0:T(8,128)(2,1)} collective-permute-done((bf16[384,1152]{1,0:T(8,128)(2,1)}, bf16[384,1152]{1,0:T(8,128)(2,1)}, u32[]{:S(2)}, u32[]{:S(2)}) %collective-permute-start) | collective-permute-done | bytes 884768 | tf_op jit(solution)/shard_map/ppermute | solution.py:14
  38.1 1.4 %fusion.2 = f32[384]{0:T(512)S(1)} fusion(bf16[384,1152]{1,0:T(8,128)(2,1)} %collective-permute-done), kind=kLoop, calls=%fused_computation.14 | loop fusion | flops 1326720 | bytes 886272 | tf_op jit(solution)/shard_map/reduce_sum | solution.py:19
  39.5 2.2 %fusion.19 = (f32[384]{0:T(512)S(1)}, f32[384,384]{0,1:T(8,128)S(1)}) fusion(f32[]{:T(128)} %bitcast.10, f32[]{:T(128)} %bitcast.7, bf16[384,1152]{1,0:T(8,128)(2,1)} %collective-permute-done, f32[384]{0:T(512)S(1)} %add_rsqrt_fusion.1, bf16[384,1152]{1,0:T(8,128)(2,1)S(1)} %copy-done.1, f32[384]{0:T(512)S(1)} %get-tuple-element.12), kind=kOutput, calls=%fused_computation.39 | convolution fusion | flops 343719552 | bytes 2363912 | tf_op jit(solution)/shard_map/dot_general | solution.py:24
  41.7 9.5 %collective-permute-done.1 = bf16[384,1152]{1,0:T(8,128)(2,1)} collective-permute-done((bf16[384,1152]{1,0:T(8,128)(2,1)}, bf16[384,1152]{1,0:T(8,128)(2,1)}, u32[]{:S(2)}, u32[]{:S(2)}) %collective-permute-start.1) | collective-permute-done | bytes 884768 | tf_op jit(solution)/shard_map/ppermute | solution.py:14
  51.2 1.4 %fusion.4 = f32[384]{0:T(512)S(1)} fusion(bf16[384,1152]{1,0:T(8,128)(2,1)} %collective-permute-done.1), kind=kLoop, calls=%fused_computation.16 | loop fusion | flops 1326720 | bytes 886272 | tf_op jit(solution)/shard_map/reduce_sum | solution.py:19
  52.6 2.2 %fusion.20 = (f32[384]{0:T(512)S(1)}, f32[384,384]{0,1:T(8,128)S(1)}) fusion(f32[]{:T(128)} %bitcast.9, f32[]{:T(128)} %bitcast.6, bf16[384,1152]{1,0:T(8,128)(2,1)} %collective-permute-done.1, f32[384]{0:T(512)S(1)} %add_rsqrt_fusion, bf16[384,1152]{1,0:T(8,128)(2,1)S(1)} %copy-done.1, f32[384]{0:T(512)S(1)} %get-tuple-element.12), kind=kOutput, calls=%fused_computation.40 | convolution fusion | flops 343719552 | bytes 2363912 | tf_op jit(solution)/shard_map/dot_general | solution.py:24
  54.9 2.0 %convolution_add_fusion.1 = f32[384,1152]{1,0:T(8,128)S(1)} fusion(f32[384,1152]{1,0:T(8,128)S(1)} %fusion.33, bf16[384,1152]{1,0:T(8,128)(2,1)} %collective-permute-done, f32[384]{0:T(512)S(1)} %add_rsqrt_fusion.1, f32[384,384]{0,1:T(8,128)S(1)} %get-tuple-element.14, f32[]{:T(128)S(6)} %mul.146), kind=kOutput, calls=%fused_computation.1 | convolution fusion | flops 342245376 | bytes 5015044 | tf_op jit(solution)/shard_map/dot_general | solution.py:131
  56.8 2.2 %fusion.11 = (f32[384]{0:T(512)S(1)}, f32[384,1152]{1,0:T(8,128)S(1)}) fusion(bf16[384,1152]{1,0:T(8,128)(2,1)S(1)} %copy-done.1, f32[384,1152]{1,0:T(8,128)S(1)} %convolution_add_fusion.1, bf16[384,1152]{1,0:T(8,128)(2,1)} %collective-permute-done.1, f32[384]{0:T(512)S(1)} %add_rsqrt_fusion, f32[384,384]{0,1:T(8,128)S(1)} %get-tuple-element.18, f32[]{:T(128)S(6)} %mul.146), kind=kOutput, calls=%fused_computation.23 | convolution fusion | flops 343572096 | bytes 5901316 | tf_op jit(solution)/shard_map/dot_general | solution.py:132
  59.1 1.3 %fusion.10 = bf16[384,1152]{1,0:T(8,128)(2,1)} fusion(bf16[384,1152]{1,0:T(8,128)(2,1)S(1)} %copy-done.1, f32[384,1152]{1,0:T(8,128)S(1)} %get-tuple-element.20, f32[384]{0:T(512)S(1)} %get-tuple-element.19, f32[384]{0:T(512)S(1)} %get-tuple-element.11, f32[384]{0:T(512)S(1)} %get-tuple-element.12), kind=kLoop, calls=%fused_computation.22 | loop fusion | flops 2654208 | bytes 3543552 | tf_op jit(solution)/shard_map/convert_element_type | solution.py:37
  60.4 24.9 %collective-permute-done.3.raw_ref = bf16[384,1152]{1,0:T(8,128)(2,1)} collective-permute-done((bf16[384,1152]{1,0:T(8,128)(2,1)}, bf16[384,1152]{1,0:T(8,128)(2,1)}, u32[]{:S(2)}, u32[]{:S(2)}) %collective-permute-start.3) | collective-permute-done | bytes 884768 | tf_op jit(solution)/shard_map/ppermute | solution.py:14
  85.3 3.0 %shard_map.76.base_ref = f32[384,1152]{1,0:T(8,128)S(1)} custom-call(f32[1]{0:T(128)} %copy.10.scale_ref, f32[1]{0:T(128)} %copy.11.bias_ref, bf16[384,1152]{1,0:T(8,128)(2,1)} %collective-permute-done.3.raw_ref, bf16[384,1152]{1,0:T(8,128)(2,1)S(1)} %fusion.1.unit_ref, f32[384,1152]{1,0:T(8,128)S(1)} %fusion.31.total_ref, bf16[384,1152]{1,0:T(8,128)(2,1)S(1)} %copy-done, ...), custom_call_target="tpu_custom_call" | custom-call | flops 679477248 | bytes 5308416 | tf_op jit(solution)/shard_map/pallas_call | solution.py:94
  88.3 0.6 add_multiply_fusion
  88.9 5.0 %collective-permute-done.2.raw_ref = bf16[384,1152]{1,0:T(8,128)(2,1)S(1)} collective-permute-done((bf16[384,1152]{1,0:T(8,128)(2,1)}, bf16[384,1152]{1,0:T(8,128)(2,1)S(1)}, u32[]{:S(2)}, u32[]{:S(2)}) %collective-permute-start.2) | collective-permute-done | bytes 884768 | tf_op jit(solution)/shard_map/ppermute | solution.py:14
  93.9 2.3 %shard_map.77 = bf16[384,1152]{1,0:T(8,128)(2,1)} custom-call(f32[1]{0:T(128)} %copy.10.scale_ref, f32[1]{0:T(128)} %copy.11.bias_ref, bf16[384,1152]{1,0:T(8,128)(2,1)S(1)} %collective-permute-done.2.raw_ref, bf16[384,1152]{1,0:T(8,128)(2,1)S(1)} %fusion.1.unit_ref, f32[384,1152]{1,0:T(8,128)S(1)} %shard_map.76.base_ref, bf16[384,1152]{1,0:T(8,128)(2,1)S(1)} %copy-done, ...), custom_call_target="tpu_custom_call" | custom-call | flops 679477248 | bytes 5308416 | tf_op jit(solution)/shard_map/pallas_call | solution.py:94
  (5 shorter events, 0.1 us)
Async XLA Ops:
  0.6 23.0 %copy-start = (bf16[384,1152]{1,0:T(8,128)(2,1)S(1)}, bf16[384,1152]{1,0:T(8,128)(2,1)}, u32[]{:S(2)}) copy-start(bf16[384,1152]{1,0:T(8,128)(2,1)} %text_ref.3) | copy-start | bytes 2654212
  0.6 24.6 %copy-start.2 = (s32[1,384]{1,0:T(1,128)S(1)}, s32[1,384]{1,0:T(1,128)}, u32[]{:S(2)}) copy-start(s32[1,384]{1,0:T(1,128)} %param.7) | copy-start | bytes 4612
  0.7 37.4 %collective-permute-start = (bf16[384,1152]{1,0:T(8,128)(2,1)}, bf16[384,1152]{1,0:T(8,128)(2,1)}, u32[]{:S(2)}, u32[]{:S(2)}) collective-permute-start(bf16[384,1152]{1,0:T(8,128)(2,1)} %text_ref.3), channel_id=1, source_target_pairs={{0,16},{1,17},{2,18},{3,19},{4,20},{5,21},{6,22},{7,23},{8,24},{9,... | collective-permute-start | bytes 2654216 | tf_op jit(solution)/shard_map/ppermute | solution.py:14
  9.1 42.1 %collective-permute-start.1 = (bf16[384,1152]{1,0:T(8,128)(2,1)}, bf16[384,1152]{1,0:T(8,128)(2,1)}, u32[]{:S(2)}, u32[]{:S(2)}) collective-permute-start(bf16[384,1152]{1,0:T(8,128)(2,1)} %text_ref.3), channel_id=1, source_target_pairs={{0,512},{32,544},{64,576},{96,608},{128,640},{160,672},{192,704},{... | collective-permute-start | bytes 2654216 | tf_op jit(solution)/shard_map/ppermute | solution.py:14
  11.5 73.8 %collective-permute-start.3 = (bf16[384,1152]{1,0:T(8,128)(2,1)}, bf16[384,1152]{1,0:T(8,128)(2,1)}, u32[]{:S(2)}, u32[]{:S(2)}) collective-permute-start(bf16[384,1152]{1,0:T(8,128)(2,1)} %param.5), channel_id=1, source_target_pairs={{0,16},{1,17},{2,18},{3,19},{4,20},{5,21},{6,22},{7,23},{8,24},{9,... | collective-permute-start | bytes 2654216 | tf_op jit(solution)/shard_map/ppermute | solution.py:14
  13.4 80.5 %collective-permute-start.2 = (bf16[384,1152]{1,0:T(8,128)(2,1)}, bf16[384,1152]{1,0:T(8,128)(2,1)S(1)}, u32[]{:S(2)}, u32[]{:S(2)}) collective-permute-start(bf16[384,1152]{1,0:T(8,128)(2,1)} %param.5), channel_id=1, source_target_pairs={{0,512},{32,544},{64,576},{96,608},{128,640},{160,672},{192,704},{... | collective-permute-start | bytes 2654216 | tf_op jit(solution)/shard_map/ppermute | solution.py:14
  25.3 2.4 %copy-start.1 = (bf16[384,1152]{1,0:T(8,128)(2,1)S(1)}, bf16[384,1152]{1,0:T(8,128)(2,1)}, u32[]{:S(2)}) copy-start(bf16[384,1152]{1,0:T(8,128)(2,1)} %param.5) | copy-start | bytes 2654212

commit v6 on v5

--- a/solution.py
+++ b/solution.py
@@ -44,7 +44,7 @@
 
 
 def plain_weight(dots, scale, bias):
-    return (scale * jax.nn.sigmoid(dots * scale + bias)).astype(jnp.bfloat16)
+    return scale * jax.nn.sigmoid(dots * scale + bias)
 
 
 def dot_rows(left, right):
@@ -56,7 +56,7 @@
 def cross_weight(scale_ref, bias_ref, raw_ref, unit_ref):
     other = unit_rows(raw_ref[...])[0]
     dots = dot_rows(unit_ref[...], other)
-    return (other, dots, plain_weight(dots, scale_ref[0], bias_ref[0]))
+    return (other, dots, plain_weight(dots, scale_ref[0], bias_ref[0]).astype(jnp.bfloat16))
 
 
 def text_side(scale_ref, bias_ref, raw_ref, unit_ref, total_ref, text_ref, inv_ref, out_ref):
@@ -68,17 +68,21 @@
 def text_last(
     scale_ref, bias_ref, raw_ref, unit_ref, base_ref, text_ref, inv_ref, out_ref, done, sems
 ):
-    other, dots, weight = cross_weight(scale_ref, bias_ref, raw_ref, unit_ref)
+    other = raw_ref[...]
+    values = other.astype(jnp.float32)
+    theirs = lax.rsqrt(jnp.sum(values * values, axis=1) + 1e-06)[None, :]
+    dots = dot_rows(unit_ref[...], other) * theirs
+    weight = plain_weight(dots, scale_ref[0], bias_ref[0]).astype(jnp.float32)
     inv = inv_ref[...]
-    inner = jnp.sum(weight.astype(jnp.float32) * dots, axis=1, keepdims=True)
-    along = inv * inv * inner
+    along = inv * inv * jnp.sum(weight * dots, axis=1, keepdims=True)
+    weight = (weight * theirs).astype(jnp.bfloat16)
     copies = []
     for index, at in enumerate(range(0, done.shape[0], STEP)):
         rows = pl.ds(at, STEP)
         part = jnp.dot(weight[at : at + STEP], other, preferred_element_type=jnp.float32)
-        values = text_ref[rows, :].astype(jnp.float32)
+        text = text_ref[rows, :].astype(jnp.float32)
         done[rows, :] = (
-            base_ref[rows, :] + inv[at : at + STEP] * part - along[at : at + STEP] * values
+            base_ref[rows, :] + inv[at : at + STEP] * part - along[at : at + STEP] * text
         ).astype(jnp.bfloat16)
         copies.append(
             pltpu.make_async_copy(done.at[rows, :], out_ref.at[rows, :], sems.at[index])

time: 96.9 us -> 96.7 us (level)
  no operation moved by 1% of the time
where the time goes in v6:
time: 96.7 us; the launch traced here: 96.1 us
  waiting for transfers between devices  48.3 us (50%)
  starting transfers between devices  20.1 us (21%)
  matrix products  12.5 us (13%)
  other arithmetic  7.85 us (8%)
  Pallas kernels  5.22 us (5%)
  between operations  2.06 us (2%)
    ppermute x4, waiting for transfers between devices, from_partner(): return lax.ppermute(block, axis, [(at, at ^ half) for at in range(count)])  48.3 us
    ppermute x4, starting transfers between devices, from_partner(): return lax.ppermute(block, axis, [(at, at ^ half) for at in range(count)])  20.1 us
    dot_general x3, matrix products, score_block(): jnp.dot(left, right.T, preferred_element_type=jnp.float32) * scale + bias  6.82 us
    reduce_sum x4, other arithmetic, unit_rows(): inv = lax.rsqrt(jnp.sum(values * values, axis=-1, keepdims=True) + 1e-06)  5.69 us
    pallas_call x2, Pallas kernels, call(): pl.pallas_call(kernel, out_shape=out, in_specs=[smem, smem] + [vmem] * (l...  5.22 us
    dot_general x1, matrix products, per_device(): jnp.dot(weight_row, row_unit, preferred_element_type=jnp.float32)  2.21 us
    dot_general x1, matrix products, per_device(): jnp.dot(weight_col, col_unit, preferred_element_type=jnp.float32)  1.98 us
  transfers between devices with their start and end apart: 4, of which 4 were waited for; matrix products, arithmetic and copies ran while one was open for 21% of the time, Pallas kernels for 3%

profile of v6, /device:TPU:904, one launch (start us, length us, event | category | flops | bytes accessed | tf_op | source)
XLA Modules:
  0.0 96.1 jit_solution(4795195336760061474)
XLA Ops:
  0.6 0.0 copy-start
  0.6 0.0 copy-start.2
  0.7 8.4 %collective-permute-start = (bf16[384,1152]{1,0:T(8,128)(2,1)}, bf16[384,1152]{1,0:T(8,128)(2,1)}, u32[]{:S(2)}, u32[]{:S(2)}) collective-permute-start(bf16[384,1152]{1,0:T(8,128)(2,1)} %text_ref.3), channel_id=1, source_target_pairs={{0,16},{1,17},{2,18},{3,19},{4,20},{5,21},{6,22},{7,23},{8,24},{9,... | collective-permute-start | bytes 2654216 | tf_op jit(solution)/shard_map/ppermute | solution.py:14
  9.1 2.4 %collective-permute-start.1 = (bf16[384,1152]{1,0:T(8,128)(2,1)}, bf16[384,1152]{1,0:T(8,128)(2,1)}, u32[]{:S(2)}, u32[]{:S(2)}) collective-permute-start(bf16[384,1152]{1,0:T(8,128)(2,1)} %text_ref.3), channel_id=1, source_target_pairs={{0,512},{32,544},{64,576},{96,608},{128,640},{160,672},{192,704},{... | collective-permute-start | bytes 2654216 | tf_op jit(solution)/shard_map/ppermute | solution.py:14
  11.5 1.9 %collective-permute-start.3 = (bf16[384,1152]{1,0:T(8,128)(2,1)}, bf16[384,1152]{1,0:T(8,128)(2,1)}, u32[]{:S(2)}, u32[]{:S(2)}) collective-permute-start(bf16[384,1152]{1,0:T(8,128)(2,1)} %param.5), channel_id=1, source_target_pairs={{0,16},{1,17},{2,18},{3,19},{4,20},{5,21},{6,22},{7,23},{8,24},{9,... | collective-permute-start | bytes 2654216 | tf_op jit(solution)/shard_map/ppermute | solution.py:14
  13.4 7.3 %collective-permute-start.2 = (bf16[384,1152]{1,0:T(8,128)(2,1)}, bf16[384,1152]{1,0:T(8,128)(2,1)S(1)}, u32[]{:S(2)}, u32[]{:S(2)}) collective-permute-start(bf16[384,1152]{1,0:T(8,128)(2,1)} %param.5), channel_id=1, source_target_pairs={{0,512},{32,544},{64,576},{96,608},{128,640},{160,672},{192,704},{... | collective-permute-start | bytes 2654216 | tf_op jit(solution)/shard_map/ppermute | solution.py:14
  20.8 1.4 %fusion.6 = f32[384]{0:T(512)S(1)} fusion(bf16[384,1152]{1,0:T(8,128)(2,1)} %param.5), kind=kLoop, calls=%fused_computation.18 | loop fusion | flops 1326720 | bytes 886272 | tf_op jit(solution)/shard_map/reduce_sum | solution.py:19
  22.2 1.4 %fusion = f32[384]{0:T(512)S(1)} fusion(bf16[384,1152]{1,0:T(8,128)(2,1)} %text_ref.3), kind=kLoop, calls=%fused_computation.12 | loop fusion | flops 1326720 | bytes 886272 | tf_op jit(solution)/shard_map/reduce_sum | solution.py:19
  23.6 0.0 copy-done
  23.6 0.2 fusion.1.unit_ref
  23.8 0.1 rsqrt.37.inv_ref
  25.3 0.0 copy-done.2
  25.3 0.0 copy-start.1
  25.3 2.4 %fusion.18 = (f32[384]{0:T(512)S(1)}, f32[384,384]{0,1:T(8,128)S(1)}) fusion(f32[]{:T(128)} %bitcast.8, f32[]{:T(128)} %bitcast.4, bf16[384,1152]{1,0:T(8,128)(2,1)S(1)} %fusion.1.unit_ref, bf16[384,1152]{1,0:T(8,128)(2,1)} %param.5, f32[384]{0:T(512)S(1)} %get-tuple-element.12, s32[384]{0:T(512)S(1)} %reduce), kind=kOutput, calls=%fused_computation.38 | convolution fusion | flops 342982272 | bytes 2363912 | tf_op jit(solution)/shard_map/dot_general | solution.py:24
  27.7 0.0 copy-done.1
  27.7 0.8 fusion.31.total_ref
  28.5 0.7 fusion.33
  29.2 8.9 %collective-permute-done = bf16[384,1152]{1,0:T(8,128)(2,1)} collective-permute-done((bf16[384,1152]{1,0:T(8,128)(2,1)}, bf16[384,1152]{1,0:T(8,128)(2,1)}, u32[]{:S(2)}, u32[]{:S(2)}) %collective-permute-start) | collective-permute-done | bytes 884768 | tf_op jit(solution)/shard_map/ppermute | solution.py:14
  38.1 1.4 %fusion.2 = f32[384]{0:T(512)S(1)} fusion(bf16[384,1152]{1,0:T(8,128)(2,1)} %collective-permute-done), kind=kLoop, calls=%fused_computation.14 | loop fusion | flops 1326720 | bytes 886272 | tf_op jit(solution)/shard_map/reduce_sum | solution.py:19
  39.5 2.2 %fusion.19 = (f32[384]{0:T(512)S(1)}, f32[384,384]{0,1:T(8,128)S(1)}) fusion(f32[]{:T(128)} %bitcast.10, f32[]{:T(128)} %bitcast.7, bf16[384,1152]{1,0:T(8,128)(2,1)} %collective-permute-done, f32[384]{0:T(512)S(1)} %add_rsqrt_fusion.1, bf16[384,1152]{1,0:T(8,128)(2,1)S(1)} %copy-done.1, f32[384]{0:T(512)S(1)} %get-tuple-element.12), kind=kOutput, calls=%fused_computation.39 | convolution fusion | flops 343719552 | bytes 2363912 | tf_op jit(solution)/shard_map/dot_general | solution.py:24
  41.7 9.5 %collective-permute-done.1 = bf16[384,1152]{1,0:T(8,128)(2,1)} collective-permute-done((bf16[384,1152]{1,0:T(8,128)(2,1)}, bf16[384,1152]{1,0:T(8,128)(2,1)}, u32[]{:S(2)}, u32[]{:S(2)}) %collective-permute-start.1) | collective-permute-done | bytes 884768 | tf_op jit(solution)/shard_map/ppermute | solution.py:14
  51.2 1.4 %fusion.4 = f32[384]{0:T(512)S(1)} fusion(bf16[384,1152]{1,0:T(8,128)(2,1)} %collective-permute-done.1), kind=kLoop, calls=%fused_computation.16 | loop fusion | flops 1326720 | bytes 886272 | tf_op jit(solution)/shard_map/reduce_sum | solution.py:19
  52.6 2.2 %fusion.20 = (f32[384]{0:T(512)S(1)}, f32[384,384]{0,1:T(8,128)S(1)}) fusion(f32[]{:T(128)} %bitcast.9, f32[]{:T(128)} %bitcast.6, bf16[384,1152]{1,0:T(8,128)(2,1)} %collective-permute-done.1, f32[384]{0:T(512)S(1)} %add_rsqrt_fusion, bf16[384,1152]{1,0:T(8,128)(2,1)S(1)} %copy-done.1, f32[384]{0:T(512)S(1)} %get-tuple-element.12), kind=kOutput, calls=%fused_computation.40 | convolution fusion | flops 343719552 | bytes 2363912 | tf_op jit(solution)/shard_map/dot_general | solution.py:24
  54.9 2.0 %convolution_add_fusion.1 = f32[384,1152]{1,0:T(8,128)S(1)} fusion(f32[384,1152]{1,0:T(8,128)S(1)} %fusion.33, bf16[384,1152]{1,0:T(8,128)(2,1)} %collective-permute-done, f32[384]{0:T(512)S(1)} %add_rsqrt_fusion.1, f32[384,384]{0,1:T(8,128)S(1)} %get-tuple-element.14, f32[]{:T(128)S(6)} %mul.146), kind=kOutput, calls=%fused_computation.1 | convolution fusion | flops 342245376 | bytes 5015044 | tf_op jit(solution)/shard_map/dot_general | solution.py:135
  56.8 2.2 %fusion.11 = (f32[384]{0:T(512)S(1)}, f32[384,1152]{1,0:T(8,128)S(1)}) fusion(bf16[384,1152]{1,0:T(8,128)(2,1)S(1)} %copy-done.1, f32[384,1152]{1,0:T(8,128)S(1)} %convolution_add_fusion.1, bf16[384,1152]{1,0:T(8,128)(2,1)} %collective-permute-done.1, f32[384]{0:T(512)S(1)} %add_rsqrt_fusion, f32[384,384]{0,1:T(8,128)S(1)} %get-tuple-element.18, f32[]{:T(128)S(6)} %mul.146), kind=kOutput, calls=%fused_computation.23 | convolution fusion | flops 343572096 | bytes 5901316 | tf_op jit(solution)/shard_map/dot_general | solution.py:136
  59.1 1.3 %fusion.10 = bf16[384,1152]{1,0:T(8,128)(2,1)} fusion(bf16[384,1152]{1,0:T(8,128)(2,1)S(1)} %copy-done.1, f32[384,1152]{1,0:T(8,128)S(1)} %get-tuple-element.20, f32[384]{0:T(512)S(1)} %get-tuple-element.19, f32[384]{0:T(512)S(1)} %get-tuple-element.11, f32[384]{0:T(512)S(1)} %get-tuple-element.12), kind=kLoop, calls=%fused_computation.22 | loop fusion | flops 2654208 | bytes 3543552 | tf_op jit(solution)/shard_map/convert_element_type | solution.py:37
  60.4 24.9 %collective-permute-done.3.raw_ref = bf16[384,1152]{1,0:T(8,128)(2,1)} collective-permute-done((bf16[384,1152]{1,0:T(8,128)(2,1)}, bf16[384,1152]{1,0:T(8,128)(2,1)}, u32[]{:S(2)}, u32[]{:S(2)}) %collective-permute-start.3) | collective-permute-done | bytes 884768 | tf_op jit(solution)/shard_map/ppermute | solution.py:14
  85.3 3.0 %shard_map.76.base_ref = f32[384,1152]{1,0:T(8,128)S(1)} custom-call(f32[1]{0:T(128)} %copy.10.scale_ref, f32[1]{0:T(128)} %copy.11.bias_ref, bf16[384,1152]{1,0:T(8,128)(2,1)} %collective-permute-done.3.raw_ref, bf16[384,1152]{1,0:T(8,128)(2,1)S(1)} %fusion.1.unit_ref, f32[384,1152]{1,0:T(8,128)S(1)} %fusion.31.total_ref, bf16[384,1152]{1,0:T(8,128)(2,1)S(1)} %copy-done, ...), custom_call_target="tpu_custom_call" | custom-call | flops 679477248 | bytes 5308416 | tf_op jit(solution)/shard_map/pallas_call | solution.py:98
  88.3 0.6 add_multiply_fusion
  88.9 5.0 %collective-permute-done.2.raw_ref = bf16[384,1152]{1,0:T(8,128)(2,1)S(1)} collective-permute-done((bf16[384,1152]{1,0:T(8,128)(2,1)}, bf16[384,1152]{1,0:T(8,128)(2,1)S(1)}, u32[]{:S(2)}, u32[]{:S(2)}) %collective-permute-start.2) | collective-permute-done | bytes 884768 | tf_op jit(solution)/shard_map/ppermute | solution.py:14
  93.9 2.2 %shard_map.77 = bf16[384,1152]{1,0:T(8,128)(2,1)} custom-call(f32[1]{0:T(128)} %copy.10.scale_ref, f32[1]{0:T(128)} %copy.11.bias_ref, bf16[384,1152]{1,0:T(8,128)(2,1)S(1)} %collective-permute-done.2.raw_ref, bf16[384,1152]{1,0:T(8,128)(2,1)S(1)} %fusion.1.unit_ref, f32[384,1152]{1,0:T(8,128)S(1)} %shard_map.76.base_ref, bf16[384,1152]{1,0:T(8,128)(2,1)S(1)} %copy-done, ...), custom_call_target="tpu_custom_call" | custom-call | flops 679477248 | bytes 5308416 | tf_op jit(solution)/shard_map/pallas_call | solution.py:98
  (5 shorter events, 0.1 us)
Async XLA Ops:
  0.6 23.0 %copy-start = (bf16[384,1152]{1,0:T(8,128)(2,1)S(1)}, bf16[384,1152]{1,0:T(8,128)(2,1)}, u32[]{:S(2)}) copy-start(bf16[384,1152]{1,0:T(8,128)(2,1)} %text_ref.3) | copy-start | bytes 2654212
  0.6 24.6 %copy-start.2 = (s32[1,384]{1,0:T(1,128)S(1)}, s32[1,384]{1,0:T(1,128)}, u32[]{:S(2)}) copy-start(s32[1,384]{1,0:T(1,128)} %param.7) | copy-start | bytes 4612
  0.7 37.4 %collective-permute-start = (bf16[384,1152]{1,0:T(8,128)(2,1)}, bf16[384,1152]{1,0:T(8,128)(2,1)}, u32[]{:S(2)}, u32[]{:S(2)}) collective-permute-start(bf16[384,1152]{1,0:T(8,128)(2,1)} %text_ref.3), channel_id=1, source_target_pairs={{0,16},{1,17},{2,18},{3,19},{4,20},{5,21},{6,22},{7,23},{8,24},{9,... | collective-permute-start | bytes 2654216 | tf_op jit(solution)/shard_map/ppermute | solution.py:14
  9.1 42.1 %collective-permute-start.1 = (bf16[384,1152]{1,0:T(8,128)(2,1)}, bf16[384,1152]{1,0:T(8,128)(2,1)}, u32[]{:S(2)}, u32[]{:S(2)}) collective-permute-start(bf16[384,1152]{1,0:T(8,128)(2,1)} %text_ref.3), channel_id=1, source_target_pairs={{0,512},{32,544},{64,576},{96,608},{128,640},{160,672},{192,704},{... | collective-permute-start | bytes 2654216 | tf_op jit(solution)/shard_map/ppermute | solution.py:14
  11.5 73.8 %collective-permute-start.3 = (bf16[384,1152]{1,0:T(8,128)(2,1)}, bf16[384,1152]{1,0:T(8,128)(2,1)}, u32[]{:S(2)}, u32[]{:S(2)}) collective-permute-start(bf16[384,1152]{1,0:T(8,128)(2,1)} %param.5), channel_id=1, source_target_pairs={{0,16},{1,17},{2,18},{3,19},{4,20},{5,21},{6,22},{7,23},{8,24},{9,... | collective-permute-start | bytes 2654216 | tf_op jit(solution)/shard_map/ppermute | solution.py:14
  13.4 80.5 %collective-permute-start.2 = (bf16[384,1152]{1,0:T(8,128)(2,1)}, bf16[384,1152]{1,0:T(8,128)(2,1)S(1)}, u32[]{:S(2)}, u32[]{:S(2)}) collective-permute-start(bf16[384,1152]{1,0:T(8,128)(2,1)} %param.5), channel_id=1, source_target_pairs={{0,512},{32,544},{64,576},{96,608},{128,640},{160,672},{192,704},{... | collective-permute-start | bytes 2654216 | tf_op jit(solution)/shard_map/ppermute | solution.py:14
  25.3 2.4 %copy-start.1 = (bf16[384,1152]{1,0:T(8,128)(2,1)S(1)}, bf16[384,1152]{1,0:T(8,128)(2,1)}, u32[]{:S(2)}) copy-start(bf16[384,1152]{1,0:T(8,128)(2,1)} %param.5) | copy-start | bytes 2654212

commit v7 on v5

--- a/solution.py
+++ b/solution.py
@@ -72,13 +72,14 @@
     inv = inv_ref[...]
     inner = jnp.sum(weight.astype(jnp.float32) * dots, axis=1, keepdims=True)
     along = inv * inv * inner
+    weight = (weight.astype(jnp.float32) * inv).astype(jnp.bfloat16)
     copies = []
     for index, at in enumerate(range(0, done.shape[0], STEP)):
         rows = pl.ds(at, STEP)
         part = jnp.dot(weight[at : at + STEP], other, preferred_element_type=jnp.float32)
         values = text_ref[rows, :].astype(jnp.float32)
         done[rows, :] = (
-            base_ref[rows, :] + inv[at : at + STEP] * part - along[at : at + STEP] * values
+            base_ref[rows, :] + part - along[at : at + STEP] * values
         ).astype(jnp.bfloat16)
         copies.append(
             pltpu.make_async_copy(done.at[rows, :], out_ref.at[rows, :], sems.at[index])

time: 96.9 us -> 96.9 us (level)
  no operation moved by 1% of the time
where the time goes in v7:
time: 96.9 us; the launch traced here: 96.3 us
  waiting for transfers between devices  48.3 us (50%)
  starting transfers between devices  20.1 us (21%)
  matrix products  12.5 us (13%)
  other arithmetic  7.85 us (8%)
  Pallas kernels  5.38 us (6%)
  between operations  2.06 us (2%)
    ppermute x4, waiting for transfers between devices, from_partner(): return lax.ppermute(block, axis, [(at, at ^ half) for at in range(count)])  48.3 us
    ppermute x4, starting transfers between devices, from_partner(): return lax.ppermute(block, axis, [(at, at ^ half) for at in range(count)])  20.1 us
    dot_general x3, matrix products, score_block(): jnp.dot(left, right.T, preferred_element_type=jnp.float32) * scale + bias  6.82 us
    reduce_sum x4, other arithmetic, unit_rows(): inv = lax.rsqrt(jnp.sum(values * values, axis=-1, keepdims=True) + 1e-06)  5.69 us
    pallas_call x2, Pallas kernels, call(): pl.pallas_call(kernel, out_shape=out, in_specs=[smem, smem] + [vmem] * (l...  5.38 us
    dot_general x1, matrix products, per_device(): jnp.dot(weight_row, row_unit, preferred_element_type=jnp.float32)  2.21 us
    dot_general x1, matrix products, per_device(): jnp.dot(weight_col, col_unit, preferred_element_type=jnp.float32)  1.98 us
  transfers between devices with their start and end apart: 4, of which 4 were waited for; matrix products, arithmetic and copies ran while one was open for 21% of the time, Pallas kernels for 3%

profile of v7, /device:TPU:904, one launch (start us, length us, event | category | flops | bytes accessed | tf_op | source)
XLA Modules:
  0.0 96.3 jit_solution(10645599739683470581)
XLA Ops:
  0.6 0.0 copy-start
  0.6 0.0 copy-start.2
  0.7 8.4 %collective-permute-start = (bf16[384,1152]{1,0:T(8,128)(2,1)}, bf16[384,1152]{1,0:T(8,128)(2,1)}, u32[]{:S(2)}, u32[]{:S(2)}) collective-permute-start(bf16[384,1152]{1,0:T(8,128)(2,1)} %text_ref.3), channel_id=1, source_target_pairs={{0,16},{1,17},{2,18},{3,19},{4,20},{5,21},{6,22},{7,23},{8,24},{9,... | collective-permute-start | bytes 2654216 | tf_op jit(solution)/shard_map/ppermute | solution.py:14
  9.1 2.4 %collective-permute-start.1 = (bf16[384,1152]{1,0:T(8,128)(2,1)}, bf16[384,1152]{1,0:T(8,128)(2,1)}, u32[]{:S(2)}, u32[]{:S(2)}) collective-permute-start(bf16[384,1152]{1,0:T(8,128)(2,1)} %text_ref.3), channel_id=1, source_target_pairs={{0,512},{32,544},{64,576},{96,608},{128,640},{160,672},{192,704},{... | collective-permute-start | bytes 2654216 | tf_op jit(solution)/shard_map/ppermute | solution.py:14
  11.5 1.9 %collective-permute-start.3 = (bf16[384,1152]{1,0:T(8,128)(2,1)}, bf16[384,1152]{1,0:T(8,128)(2,1)}, u32[]{:S(2)}, u32[]{:S(2)}) collective-permute-start(bf16[384,1152]{1,0:T(8,128)(2,1)} %param.5), channel_id=1, source_target_pairs={{0,16},{1,17},{2,18},{3,19},{4,20},{5,21},{6,22},{7,23},{8,24},{9,... | collective-permute-start | bytes 2654216 | tf_op jit(solution)/shard_map/ppermute | solution.py:14
  13.4 7.3 %collective-permute-start.2 = (bf16[384,1152]{1,0:T(8,128)(2,1)}, bf16[384,1152]{1,0:T(8,128)(2,1)S(1)}, u32[]{:S(2)}, u32[]{:S(2)}) collective-permute-start(bf16[384,1152]{1,0:T(8,128)(2,1)} %param.5), channel_id=1, source_target_pairs={{0,512},{32,544},{64,576},{96,608},{128,640},{160,672},{192,704},{... | collective-permute-start | bytes 2654216 | tf_op jit(solution)/shard_map/ppermute | solution.py:14
  20.8 1.4 %fusion.6 = f32[384]{0:T(512)S(1)} fusion(bf16[384,1152]{1,0:T(8,128)(2,1)} %param.5), kind=kLoop, calls=%fused_computation.18 | loop fusion | flops 1326720 | bytes 886272 | tf_op jit(solution)/shard_map/reduce_sum | solution.py:19
  22.2 1.4 %fusion = f32[384]{0:T(512)S(1)} fusion(bf16[384,1152]{1,0:T(8,128)(2,1)} %text_ref.3), kind=kLoop, calls=%fused_computation.12 | loop fusion | flops 1326720 | bytes 886272 | tf_op jit(solution)/shard_map/reduce_sum | solution.py:19
  23.6 0.0 copy-done
  23.6 0.2 fusion.1.unit_ref
  23.8 0.1 rsqrt.37.inv_ref
  25.3 0.0 copy-done.2
  25.3 0.0 copy-start.1
  25.3 2.4 %fusion.18 = (f32[384]{0:T(512)S(1)}, f32[384,384]{0,1:T(8,128)S(1)}) fusion(f32[]{:T(128)} %bitcast.8, f32[]{:T(128)} %bitcast.4, bf16[384,1152]{1,0:T(8,128)(2,1)S(1)} %fusion.1.unit_ref, bf16[384,1152]{1,0:T(8,128)(2,1)} %param.5, f32[384]{0:T(512)S(1)} %get-tuple-element.12, s32[384]{0:T(512)S(1)} %reduce), kind=kOutput, calls=%fused_computation.38 | convolution fusion | flops 342982272 | bytes 2363912 | tf_op jit(solution)/shard_map/dot_general | solution.py:24
  27.7 0.0 copy-done.1
  27.7 0.8 fusion.31.total_ref
  28.5 0.7 fusion.33
  29.2 8.9 %collective-permute-done = bf16[384,1152]{1,0:T(8,128)(2,1)} collective-permute-done((bf16[384,1152]{1,0:T(8,128)(2,1)}, bf16[384,1152]{1,0:T(8,128)(2,1)}, u32[]{:S(2)}, u32[]{:S(2)}) %collective-permute-start) | collective-permute-done | bytes 884768 | tf_op jit(solution)/shard_map/ppermute | solution.py:14
  38.1 1.4 %fusion.2 = f32[384]{0:T(512)S(1)} fusion(bf16[384,1152]{1,0:T(8,128)(2,1)} %collective-permute-done), kind=kLoop, calls=%fused_computation.14 | loop fusion | flops 1326720 | bytes 886272 | tf_op jit(solution)/shard_map/reduce_sum | solution.py:19
  39.5 2.2 %fusion.19 = (f32[384]{0:T(512)S(1)}, f32[384,384]{0,1:T(8,128)S(1)}) fusion(f32[]{:T(128)} %bitcast.10, f32[]{:T(128)} %bitcast.7, bf16[384,1152]{1,0:T(8,128)(2,1)} %collective-permute-done, f32[384]{0:T(512)S(1)} %add_rsqrt_fusion.1, bf16[384,1152]{1,0:T(8,128)(2,1)S(1)} %copy-done.1, f32[384]{0:T(512)S(1)} %get-tuple-element.12), kind=kOutput, calls=%fused_computation.39 | convolution fusion | flops 343719552 | bytes 2363912 | tf_op jit(solution)/shard_map/dot_general | solution.py:24
  41.7 9.5 %collective-permute-done.1 = bf16[384,1152]{1,0:T(8,128)(2,1)} collective-permute-done((bf16[384,1152]{1,0:T(8,128)(2,1)}, bf16[384,1152]{1,0:T(8,128)(2,1)}, u32[]{:S(2)}, u32[]{:S(2)}) %collective-permute-start.1) | collective-permute-done | bytes 884768 | tf_op jit(solution)/shard_map/ppermute | solution.py:14
  51.2 1.4 %fusion.4 = f32[384]{0:T(512)S(1)} fusion(bf16[384,1152]{1,0:T(8,128)(2,1)} %collective-permute-done.1), kind=kLoop, calls=%fused_computation.16 | loop fusion | flops 1326720 | bytes 886272 | tf_op jit(solution)/shard_map/reduce_sum | solution.py:19
  52.6 2.2 %fusion.20 = (f32[384]{0:T(512)S(1)}, f32[384,384]{0,1:T(8,128)S(1)}) fusion(f32[]{:T(128)} %bitcast.9, f32[]{:T(128)} %bitcast.6, bf16[384,1152]{1,0:T(8,128)(2,1)} %collective-permute-done.1, f32[384]{0:T(512)S(1)} %add_rsqrt_fusion, bf16[384,1152]{1,0:T(8,128)(2,1)S(1)} %copy-done.1, f32[384]{0:T(512)S(1)} %get-tuple-element.12), kind=kOutput, calls=%fused_computation.40 | convolution fusion | flops 343719552 | bytes 2363912 | tf_op jit(solution)/shard_map/dot_general | solution.py:24
  54.9 2.0 %convolution_add_fusion.1 = f32[384,1152]{1,0:T(8,128)S(1)} fusion(f32[384,1152]{1,0:T(8,128)S(1)} %fusion.33, bf16[384,1152]{1,0:T(8,128)(2,1)} %collective-permute-done, f32[384]{0:T(512)S(1)} %add_rsqrt_fusion.1, f32[384,384]{0,1:T(8,128)S(1)} %get-tuple-element.14, f32[]{:T(128)S(6)} %mul.146), kind=kOutput, calls=%fused_computation.1 | convolution fusion | flops 342245376 | bytes 5015044 | tf_op jit(solution)/shard_map/dot_general | solution.py:132
  56.8 2.2 %fusion.11 = (f32[384]{0:T(512)S(1)}, f32[384,1152]{1,0:T(8,128)S(1)}) fusion(bf16[384,1152]{1,0:T(8,128)(2,1)S(1)} %copy-done.1, f32[384,1152]{1,0:T(8,128)S(1)} %convolution_add_fusion.1, bf16[384,1152]{1,0:T(8,128)(2,1)} %collective-permute-done.1, f32[384]{0:T(512)S(1)} %add_rsqrt_fusion, f32[384,384]{0,1:T(8,128)S(1)} %get-tuple-element.18, f32[]{:T(128)S(6)} %mul.146), kind=kOutput, calls=%fused_computation.23 | convolution fusion | flops 343572096 | bytes 5901316 | tf_op jit(solution)/shard_map/dot_general | solution.py:133
  59.1 1.3 %fusion.10 = bf16[384,1152]{1,0:T(8,128)(2,1)} fusion(bf16[384,1152]{1,0:T(8,128)(2,1)S(1)} %copy-done.1, f32[384,1152]{1,0:T(8,128)S(1)} %get-tuple-element.20, f32[384]{0:T(512)S(1)} %get-tuple-element.19, f32[384]{0:T(512)S(1)} %get-tuple-element.11, f32[384]{0:T(512)S(1)} %get-tuple-element.12), kind=kLoop, calls=%fused_computation.22 | loop fusion | flops 2654208 | bytes 3543552 | tf_op jit(solution)/shard_map/convert_element_type | solution.py:37
  60.4 24.9 %collective-permute-done.3.raw_ref = bf16[384,1152]{1,0:T(8,128)(2,1)} collective-permute-done((bf16[384,1152]{1,0:T(8,128)(2,1)}, bf16[384,1152]{1,0:T(8,128)(2,1)}, u32[]{:S(2)}, u32[]{:S(2)}) %collective-permute-start.3) | collective-permute-done | bytes 884768 | tf_op jit(solution)/shard_map/ppermute | solution.py:14
  85.3 3.0 %shard_map.76.base_ref = f32[384,1152]{1,0:T(8,128)S(1)} custom-call(f32[1]{0:T(128)} %copy.10.scale_ref, f32[1]{0:T(128)} %copy.11.bias_ref, bf16[384,1152]{1,0:T(8,128)(2,1)} %collective-permute-done.3.raw_ref, bf16[384,1152]{1,0:T(8,128)(2,1)S(1)} %fusion.1.unit_ref, f32[384,1152]{1,0:T(8,128)S(1)} %fusion.31.total_ref, bf16[384,1152]{1,0:T(8,128)(2,1)S(1)} %copy-done, ...), custom_call_target="tpu_custom_call" | custom-call | flops 679477248 | bytes 5308416 | tf_op jit(solution)/shard_map/pallas_call | solution.py:95
  88.3 0.6 add_multiply_fusion
  88.9 5.0 %collective-permute-done.2.raw_ref = bf16[384,1152]{1,0:T(8,128)(2,1)S(1)} collective-permute-done((bf16[384,1152]{1,0:T(8,128)(2,1)}, bf16[384,1152]{1,0:T(8,128)(2,1)S(1)}, u32[]{:S(2)}, u32[]{:S(2)}) %collective-permute-start.2) | collective-permute-done | bytes 884768 | tf_op jit(solution)/shard_map/ppermute | solution.py:14
  93.9 2.3 %shard_map.77 = bf16[384,1152]{1,0:T(8,128)(2,1)} custom-call(f32[1]{0:T(128)} %copy.10.scale_ref, f32[1]{0:T(128)} %copy.11.bias_ref, bf16[384,1152]{1,0:T(8,128)(2,1)S(1)} %collective-permute-done.2.raw_ref, bf16[384,1152]{1,0:T(8,128)(2,1)S(1)} %fusion.1.unit_ref, f32[384,1152]{1,0:T(8,128)S(1)} %shard_map.76.base_ref, bf16[384,1152]{1,0:T(8,128)(2,1)S(1)} %copy-done, ...), custom_call_target="tpu_custom_call" | custom-call | flops 679477248 | bytes 5308416 | tf_op jit(solution)/shard_map/pallas_call | solution.py:95
  (5 shorter events, 0.1 us)
Async XLA Ops:
  0.6 23.0 %copy-start = (bf16[384,1152]{1,0:T(8,128)(2,1)S(1)}, bf16[384,1152]{1,0:T(8,128)(2,1)}, u32[]{:S(2)}) copy-start(bf16[384,1152]{1,0:T(8,128)(2,1)} %text_ref.3) | copy-start | bytes 2654212
  0.6 24.6 %copy-start.2 = (s32[1,384]{1,0:T(1,128)S(1)}, s32[1,384]{1,0:T(1,128)}, u32[]{:S(2)}) copy-start(s32[1,384]{1,0:T(1,128)} %param.7) | copy-start | bytes 4612
  0.7 37.4 %collective-permute-start = (bf16[384,1152]{1,0:T(8,128)(2,1)}, bf16[384,1152]{1,0:T(8,128)(2,1)}, u32[]{:S(2)}, u32[]{:S(2)}) collective-permute-start(bf16[384,1152]{1,0:T(8,128)(2,1)} %text_ref.3), channel_id=1, source_target_pairs={{0,16},{1,17},{2,18},{3,19},{4,20},{5,21},{6,22},{7,23},{8,24},{9,... | collective-permute-start | bytes 2654216 | tf_op jit(solution)/shard_map/ppermute | solution.py:14
  9.1 42.1 %collective-permute-start.1 = (bf16[384,1152]{1,0:T(8,128)(2,1)}, bf16[384,1152]{1,0:T(8,128)(2,1)}, u32[]{:S(2)}, u32[]{:S(2)}) collective-permute-start(bf16[384,1152]{1,0:T(8,128)(2,1)} %text_ref.3), channel_id=1, source_target_pairs={{0,512},{32,544},{64,576},{96,608},{128,640},{160,672},{192,704},{... | collective-permute-start | bytes 2654216 | tf_op jit(solution)/shard_map/ppermute | solution.py:14
  11.5 73.8 %collective-permute-start.3 = (bf16[384,1152]{1,0:T(8,128)(2,1)}, bf16[384,1152]{1,0:T(8,128)(2,1)}, u32[]{:S(2)}, u32[]{:S(2)}) collective-permute-start(bf16[384,1152]{1,0:T(8,128)(2,1)} %param.5), channel_id=1, source_target_pairs={{0,16},{1,17},{2,18},{3,19},{4,20},{5,21},{6,22},{7,23},{8,24},{9,... | collective-permute-start | bytes 2654216 | tf_op jit(solution)/shard_map/ppermute | solution.py:14
  13.4 80.5 %collective-permute-start.2 = (bf16[384,1152]{1,0:T(8,128)(2,1)}, bf16[384,1152]{1,0:T(8,128)(2,1)S(1)}, u32[]{:S(2)}, u32[]{:S(2)}) collective-permute-start(bf16[384,1152]{1,0:T(8,128)(2,1)} %param.5), channel_id=1, source_target_pairs={{0,512},{32,544},{64,576},{96,608},{128,640},{160,672},{192,704},{... | collective-permute-start | bytes 2654216 | tf_op jit(solution)/shard_map/ppermute | solution.py:14
  25.3 2.4 %copy-start.1 = (bf16[384,1152]{1,0:T(8,128)(2,1)S(1)}, bf16[384,1152]{1,0:T(8,128)(2,1)}, u32[]{:S(2)}) copy-start(bf16[384,1152]{1,0:T(8,128)(2,1)} %param.5) | copy-start | bytes 2654212
